TPU v7x, 128 devices: a whole 4x4x4 slice. The times are simulated.
128 devices in a mesh: row: 8 (over y_lo, x), col: 16 (over y_hi, z, core).
Axes of the slice: x: 4, y: 4 (y_hi: 2, y_lo: 2; y = y_hi * 2 + y_lo), z: 4, core: 2. Of those that a mesh axis runs over, the one named last changes fastest.
Arguments:
- photo_vectors: float32 [16384, 1152], P(('row', 'col')), may hold values from -60 to 60
- sentence_vectors: float32 [16384, 1152], P(('row', 'col')), may hold values from -60 to 60
- matching_index: int32 [16384], replicated, may hold values from 0 to 16383, each once
- natural_warmth_exponent: float32 [1], replicated, may hold values from 4 to 4.8
- shift_term: float32 [1], replicated, may hold values from -4 to -1
Outputs:
- image_grad: float32 [16384, 1152], P(('row', 'col'))
- text_grad: float32 [16384, 1152], P(('row', 'col'))
Inputs may be any that keep to these rules, and one draw needn't show every extreme that they name: `matching_index`: every text index appears exactly once.
All inputs are finite; a program needn't handle non-finite values.
Results may differ from a plain program's by a relative error of at most 0.0003.
Values sent between devices are 32-bit elements; how exact they have to be, the bound alone decides.
No kernel may reach another device: no remote copies, remote signals or barrier semaphores. Data moves between devices by JAX's collectives and lax.ppermute only.
A program may use at most 64 MiB of HBM per device.

v0:
```python
import jax
import jax.numpy as jnp
from jax import lax
from jax.sharding import PartitionSpec as P

epsilon = 1e-06


def from_behind(value, axis, steps):
    count = lax.axis_size(axis)
    pairs = [(source, (source + steps) % count) for source in range(count)]
    return lax.ppermute(value, axis, pairs)


def normalize(raw):
    squares = jnp.sum(raw * raw, axis=-1, keepdims=True)
    length = jnp.sqrt(squares + epsilon)
    return (raw / length, length)


def restore_grad(d_unit, unit_vec, length):
    along = jnp.sum(unit_vec * d_unit, axis=-1, keepdims=True)
    return (d_unit - unit_vec * along) / length


def pair_gradients(
    photo_batch,
    matching_indices,
    sentence_tile,
    vertical_values,
    warmth_multiplier,
    tile_start_index,
):
    similarity_matrix = (
        warmth_multiplier
        * lax.dot_general(
            photo_batch,
            sentence_tile,
            (((1,), (1,)), ((), ())),
            precision=lax.Precision.HIGHEST,
            preferred_element_type=jnp.float32,
        )
        + tile_start_index
    )
    labels = jnp.where(
        matching_indices[:, None] == vertical_values[None, :], jnp.float32(1.0), jnp.float32(-1.0)
    )
    similarity_derivative = -labels * jax.nn.sigmoid(-labels * similarity_matrix)
    batch_derivative = warmth_multiplier * jnp.dot(
        similarity_derivative,
        sentence_tile,
        precision=lax.Precision.HIGHEST,
        preferred_element_type=jnp.float32,
    )
    tile_derivative = warmth_multiplier * lax.dot_general(
        similarity_derivative,
        photo_batch,
        (((0,), (0,)), ((), ())),
        precision=lax.Precision.HIGHEST,
        preferred_element_type=jnp.float32,
    )
    return (batch_derivative, tile_derivative)


def per_device(
    photo_vectors, sentence_vectors, matching_index, natural_warmth_exponent, shift_term
):
    row_count = photo_vectors.shape[0]
    feat_count = photo_vectors.shape[1]
    row_size = lax.axis_size("row")
    col_size = lax.axis_size("col")
    rank_row = lax.axis_index("row")
    rank_col = lax.axis_index("col")
    warmth_multiplier = jnp.exp(natural_warmth_exponent[0])
    tile_start_index = shift_term[0]
    img_unit, img_len = normalize(photo_vectors)
    sentence_normed, txt_len = normalize(sentence_vectors)
    photo_batch = lax.all_gather(img_unit, "row", axis=0, tiled=True)
    target_grid = matching_index.reshape(row_size, col_size, row_count)
    matching_indices = lax.dynamic_slice_in_dim(target_grid, rank_col, 1, 1).reshape(
        row_size * row_count
    )
    back_block = sentence_normed[row_count:]
    forward = (sentence_normed, jnp.zeros(sentence_normed.shape, jnp.float32))
    backward = (back_block, jnp.zeros(back_block.shape, jnp.float32))
    slot_sums = jnp.zeros((1, feat_count), jnp.float32)
    group_sums = jnp.zeros(photo_batch.shape, jnp.float32)

    def visit(step, forward, backward, group_sums, slot_sums):
        from_fore = (rank_col - step) % col_size
        from_back = (rank_col + step) % col_size
        fore_start = (rank_row * col_size + from_fore) * row_count
        back_start = (rank_row * col_size + from_back) * row_count + row_count
        sentence_tile = jnp.concatenate([forward[0], backward[0]], axis=0)
        vertical_values = jnp.concatenate(
            [
                fore_start + jnp.arange(row_count, dtype=jnp.int32),
                back_start + jnp.arange(row_count - row_count, dtype=jnp.int32),
            ]
        )
        batch_derivative, tile_derivative = pair_gradients(
            photo_batch,
            matching_indices,
            sentence_tile,
            vertical_values,
            warmth_multiplier,
            tile_start_index,
        )
        group_sums = group_sums + batch_derivative
        forward = (forward[0], forward[1] + tile_derivative)
        backward = (backward[0], backward[1] + tile_derivative[row_count:])
        return (forward, backward, group_sums, slot_sums)

    def turn(step, state):
        forward, backward, group_sums, slot_sums = state
        forward = from_behind((forward[0], forward[1]), "col", 1)
        return visit(step, tuple(forward), tuple(backward), group_sums, slot_sums)

    state = visit(jnp.int32(0), forward, backward, group_sums, slot_sums)
    forward, backward, group_sums, slot_sums = lax.fori_loop(1, col_size, turn, state)
    photo_derivative = lax.psum_scatter(group_sums, "row", scatter_dimension=0, tiled=True)
    fore_grad = from_behind(forward[1], "col", 1)
    back_grad = backward[1]
    sentence_derivative = jnp.concatenate([fore_grad, back_grad], axis=0)
    return (
        restore_grad(photo_derivative, img_unit, img_len),
        restore_grad(sentence_derivative, sentence_normed, txt_len),
    )


def solution(mesh):
    return jax.shard_map(
        per_device,
        mesh=mesh,
        in_specs=(P(("row", "col"), None), P(("row", "col"), None), P(), P(), P()),
        out_specs=(P(("row", "col"), None), P(("row", "col"), None)),
        check_vma=False,
    )
```

profile of v0, /device:TPU:0, one launch (start us, length us, event | category | flops | bytes accessed | tf_op | source)
XLA Modules:
  0.0 619.3 jit_solution(1467745115641657347)
XLA Ops:
  14.3 56.3 %all-gather.2.cloned.1.call-done = f32[1024,1152]{1,0:T(8,128)} async-done(((f32[128,1152]{1,0:T(8,128)}), f32[1024,1152]{1,0:T(8,128)}) %all-gather.2.cloned.1.call-update) | async-done | bytes 4718608 | tf_op jit(solution)/shard_map/all_gather | solution.py:78
  85.3 469.5 %while.19 = (s32[]{:T(128)}, f32[128,1152]{1,0:T(8,128)S(1)}, f32[128,1152]{1,0:T(8,128)S(1)}, f32[1024,1152]{1,0:T(8,128)}, f32[]{:T(128)}, /*index=5*/s32[8,1,...) while((s32[]{:T(128)}, f32[128,1152]{1,0:T(8,128)S(1)}, ...), condition=%wide.region_3.4_spmd, body=%wide.region_2.3_spmd.sunk | while | flops 5439782912 | bytes 80614888 | solution.py:120
  87.2 11.2 %collective-permute-done = f32[128,1152]{1,0:T(8,128)S(1)} collective-permute-done((f32[128,1152]{1,0:T(8,128)S(1)}, f32[128,1152]{1,0:T(8,128)S(1)}, u32[]{:S(2)}, u32[]{:S(2)}) %collective-permute-start) | collective-permute-done | bytes 589856 | tf_op jit(solution)/shard_map/while/body/eval_jaxpr/ppermute | solution.py:12
  116.8 12.9 %collective-permute-done = f32[128,1152]{1,0:T(8,128)S(1)} collective-permute-done((f32[128,1152]{1,0:T(8,128)S(1)}, f32[128,1152]{1,0:T(8,128)S(1)}, u32[]{:S(2)}, u32[]{:S(2)}) %collective-permute-start) | collective-permute-done | bytes 589856 | tf_op jit(solution)/shard_map/while/body/eval_jaxpr/ppermute | solution.py:12
  129.8 7.3 %fusion.43 = f32[1024,128]{1,0:T(8,128)S(1)} fusion(f32[1024,1152]{1,0:T(8,128)} %get-tuple-element.369, f32[128,1152]{1,0:T(8,128)S(1)} %collective-permute-done, f32[]{:T(128)} %get-tuple-element.370, f32[]{:T(128)} %get-tuple-element.365, s32[128]{0:T(128)S(1)} %iota_add_fusion.3, s32[1024]{0:T(1024)S(1)} %bitcast.38), kind=kOutput, calls=%fused_computation.11.clone.1 | convolution fusion | flops 1813250048 | bytes 5837320 | tf_op jit(solution)/shard_map/while/body/eval_jaxpr/dot_general | solution.py:36
  148.1 12.9 %collective-permute-done = f32[128,1152]{1,0:T(8,128)S(1)} collective-permute-done((f32[128,1152]{1,0:T(8,128)S(1)}, f32[128,1152]{1,0:T(8,128)S(1)}, u32[]{:S(2)}, u32[]{:S(2)}) %collective-permute-start) | collective-permute-done | bytes 589856 | tf_op jit(solution)/shard_map/while/body/eval_jaxpr/ppermute | solution.py:12
  161.1 7.3 %fusion.43 = f32[1024,128]{1,0:T(8,128)S(1)} fusion(f32[1024,1152]{1,0:T(8,128)} %get-tuple-element.369, f32[128,1152]{1,0:T(8,128)S(1)} %collective-permute-done, f32[]{:T(128)} %get-tuple-element.370, f32[]{:T(128)} %get-tuple-element.365, s32[128]{0:T(128)S(1)} %iota_add_fusion.3, s32[1024]{0:T(1024)S(1)} %bitcast.38), kind=kOutput, calls=%fused_computation.11.clone.1 | convolution fusion | flops 1813250048 | bytes 5837320 | tf_op jit(solution)/shard_map/while/body/eval_jaxpr/dot_general | solution.py:36
  179.4 12.9 %collective-permute-done = f32[128,1152]{1,0:T(8,128)S(1)} collective-permute-done((f32[128,1152]{1,0:T(8,128)S(1)}, f32[128,1152]{1,0:T(8,128)S(1)}, u32[]{:S(2)}, u32[]{:S(2)}) %collective-permute-start) | collective-permute-done | bytes 589856 | tf_op jit(solution)/shard_map/while/body/eval_jaxpr/ppermute | solution.py:12
  192.3 7.3 %fusion.43 = f32[1024,128]{1,0:T(8,128)S(1)} fusion(f32[1024,1152]{1,0:T(8,128)} %get-tuple-element.369, f32[128,1152]{1,0:T(8,128)S(1)} %collective-permute-done, f32[]{:T(128)} %get-tuple-element.370, f32[]{:T(128)} %get-tuple-element.365, s32[128]{0:T(128)S(1)} %iota_add_fusion.3, s32[1024]{0:T(1024)S(1)} %bitcast.38), kind=kOutput, calls=%fused_computation.11.clone.1 | convolution fusion | flops 1813250048 | bytes 5837320 | tf_op jit(solution)/shard_map/while/body/eval_jaxpr/dot_general | solution.py:36
  210.7 12.9 %collective-permute-done = f32[128,1152]{1,0:T(8,128)S(1)} collective-permute-done((f32[128,1152]{1,0:T(8,128)S(1)}, f32[128,1152]{1,0:T(8,128)S(1)}, u32[]{:S(2)}, u32[]{:S(2)}) %collective-permute-start) | collective-permute-done | bytes 589856 | tf_op jit(solution)/shard_map/while/body/eval_jaxpr/ppermute | solution.py:12
  223.6 7.3 %fusion.43 = f32[1024,128]{1,0:T(8,128)S(1)} fusion(f32[1024,1152]{1,0:T(8,128)} %get-tuple-element.369, f32[128,1152]{1,0:T(8,128)S(1)} %collective-permute-done, f32[]{:T(128)} %get-tuple-element.370, f32[]{:T(128)} %get-tuple-element.365, s32[128]{0:T(128)S(1)} %iota_add_fusion.3, s32[1024]{0:T(1024)S(1)} %bitcast.38), kind=kOutput, calls=%fused_computation.11.clone.1 | convolution fusion | flops 1813250048 | bytes 5837320 | tf_op jit(solution)/shard_map/while/body/eval_jaxpr/dot_general | solution.py:36
  241.9 12.9 %collective-permute-done = f32[128,1152]{1,0:T(8,128)S(1)} collective-permute-done((f32[128,1152]{1,0:T(8,128)S(1)}, f32[128,1152]{1,0:T(8,128)S(1)}, u32[]{:S(2)}, u32[]{:S(2)}) %collective-permute-start) | collective-permute-done | bytes 589856 | tf_op jit(solution)/shard_map/while/body/eval_jaxpr/ppermute | solution.py:12
  273.2 12.9 %collective-permute-done = f32[128,1152]{1,0:T(8,128)S(1)} collective-permute-done((f32[128,1152]{1,0:T(8,128)S(1)}, f32[128,1152]{1,0:T(8,128)S(1)}, u32[]{:S(2)}, u32[]{:S(2)}) %collective-permute-start) | collective-permute-done | bytes 589856 | tf_op jit(solution)/shard_map/while/body/eval_jaxpr/ppermute | solution.py:12
  304.5 12.9 %collective-permute-done = f32[128,1152]{1,0:T(8,128)S(1)} collective-permute-done((f32[128,1152]{1,0:T(8,128)S(1)}, f32[128,1152]{1,0:T(8,128)S(1)}, u32[]{:S(2)}, u32[]{:S(2)}) %collective-permute-start) | collective-permute-done | bytes 589856 | tf_op jit(solution)/shard_map/while/body/eval_jaxpr/ppermute | solution.py:12
  335.8 12.9 %collective-permute-done = f32[128,1152]{1,0:T(8,128)S(1)} collective-permute-done((f32[128,1152]{1,0:T(8,128)S(1)}, f32[128,1152]{1,0:T(8,128)S(1)}, u32[]{:S(2)}, u32[]{:S(2)}) %collective-permute-start) | collective-permute-done | bytes 589856 | tf_op jit(solution)/shard_map/while/body/eval_jaxpr/ppermute | solution.py:12
  367.1 12.9 %collective-permute-done = f32[128,1152]{1,0:T(8,128)S(1)} collective-permute-done((f32[128,1152]{1,0:T(8,128)S(1)}, f32[128,1152]{1,0:T(8,128)S(1)}, u32[]{:S(2)}, u32[]{:S(2)}) %collective-permute-start) | collective-permute-done | bytes 589856 | tf_op jit(solution)/shard_map/while/body/eval_jaxpr/ppermute | solution.py:12
  398.4 12.9 %collective-permute-done = f32[128,1152]{1,0:T(8,128)S(1)} collective-permute-done((f32[128,1152]{1,0:T(8,128)S(1)}, f32[128,1152]{1,0:T(8,128)S(1)}, u32[]{:S(2)}, u32[]{:S(2)}) %collective-permute-start) | collective-permute-done | bytes 589856 | tf_op jit(solution)/shard_map/while/body/eval_jaxpr/ppermute | solution.py:12
  411.3 7.3 %fusion.43 = f32[1024,128]{1,0:T(8,128)S(1)} fusion(f32[1024,1152]{1,0:T(8,128)} %get-tuple-element.369, f32[128,1152]{1,0:T(8,128)S(1)} %collective-permute-done, f32[]{:T(128)} %get-tuple-element.370, f32[]{:T(128)} %get-tuple-element.365, s32[128]{0:T(128)S(1)} %iota_add_fusion.3, s32[1024]{0:T(1024)S(1)} %bitcast.38), kind=kOutput, calls=%fused_computation.11.clone.1 | convolution fusion | flops 1813250048 | bytes 5837320 | tf_op jit(solution)/shard_map/while/body/eval_jaxpr/dot_general | solution.py:36
  429.7 12.9 %collective-permute-done = f32[128,1152]{1,0:T(8,128)S(1)} collective-permute-done((f32[128,1152]{1,0:T(8,128)S(1)}, f32[128,1152]{1,0:T(8,128)S(1)}, u32[]{:S(2)}, u32[]{:S(2)}) %collective-permute-start) | collective-permute-done | bytes 589856 | tf_op jit(solution)/shard_map/while/body/eval_jaxpr/ppermute | solution.py:12
  460.9 12.9 %collective-permute-done = f32[128,1152]{1,0:T(8,128)S(1)} collective-permute-done((f32[128,1152]{1,0:T(8,128)S(1)}, f32[128,1152]{1,0:T(8,128)S(1)}, u32[]{:S(2)}, u32[]{:S(2)}) %collective-permute-start) | collective-permute-done | bytes 589856 | tf_op jit(solution)/shard_map/while/body/eval_jaxpr/ppermute | solution.py:12
  492.2 12.9 %collective-permute-done = f32[128,1152]{1,0:T(8,128)S(1)} collective-permute-done((f32[128,1152]{1,0:T(8,128)S(1)}, f32[128,1152]{1,0:T(8,128)S(1)}, u32[]{:S(2)}, u32[]{:S(2)}) %collective-permute-start) | collective-permute-done | bytes 589856 | tf_op jit(solution)/shard_map/while/body/eval_jaxpr/ppermute | solution.py:12
  523.5 12.9 %collective-permute-done = f32[128,1152]{1,0:T(8,128)S(1)} collective-permute-done((f32[128,1152]{1,0:T(8,128)S(1)}, f32[128,1152]{1,0:T(8,128)S(1)}, u32[]{:S(2)}, u32[]{:S(2)}) %collective-permute-start) | collective-permute-done | bytes 589856 | tf_op jit(solution)/shard_map/while/body/eval_jaxpr/ppermute | solution.py:12
  554.9 12.9 %collective-permute-done.2 = f32[128,1152]{1,0:T(8,128)S(1)} collective-permute-done((f32[128,1152]{1,0:T(8,128)S(1)}, f32[128,1152]{1,0:T(8,128)S(1)}, u32[]{:S(2)}, u32[]{:S(2)}) %collective-permute-start.2) | collective-permute-done | bytes 589856 | tf_op jit(solution)/shard_map/ppermute | solution.py:12
  569.0 40.1 %reduce-scatter.2.cloned.1.call-done = f32[128,1152]{1,0:T(8,128)} async-done(((f32[1024,1152]{1,0:T(8,128)}), f32[128,1152]{1,0:T(8,128)}) %reduce-scatter.2.cloned.1.call-update) | async-done | bytes 589840 | tf_op jit(solution)/shard_map/reduce_scatter | solution.py:121
  (281 shorter events, 264.5 us)
Async XLA Ops:
  7.2 63.4 %all-gather.2.cloned.1.call-start = ((), (), s32[]{:S(2)}) async-start(), calls=%async_computation.1 | async-start | bytes 5308416 | tf_op jit(solution)/shard_map/all_gather | solution.py:78
  10.4 598.7 %reduce-scatter.2.cloned.1.call-start = ((), (), s32[]{:S(2)}) async-start(), calls=%async_computation.2 | async-start | bytes 5308416 | tf_op jit(solution)/shard_map/reduce_scatter | solution.py:121
  85.4 13.0 %collective-permute-start = (f32[128,1152]{1,0:T(8,128)S(1)}, f32[128,1152]{1,0:T(8,128)S(1)}, u32[]{:S(2)}, u32[]{:S(2)}) collective-permute-start(f32[128,1152]{1,0:T(8,128)S(1)} %get-tuple-element.347), channel_id=1, source_target_pairs={{0,1},{1,2},{2,3},{3,4},{4,5},{5,6},{6,7},{7,8},{8,9},{9,10},{10,1... | collective-permute-start | bytes 1769480 | tf_op jit(solution)/shard_map/while/body/eval_jaxpr/ppermute | solution.py:12
  85.5 20.3 %collective-permute-start.1 = (f32[128,1152]{1,0:T(8,128)S(1)}, f32[128,1152]{1,0:T(8,128)S(1)}, u32[]{:S(2)}, u32[]{:S(2)}) collective-permute-start(f32[128,1152]{1,0:T(8,128)S(1)} %get-tuple-element.348), channel_id=1, source_target_pairs={{0,1},{1,2},{2,3},{3,4},{4,5},{5,6},{6,7},{7,8},{8,9},{9,10},{10,1... | collective-permute-start | bytes 1769480 | tf_op jit(solution)/shard_map/while/body/eval_jaxpr/ppermute | solution.py:12
  116.8 20.3 %collective-permute-start.1 = (f32[128,1152]{1,0:T(8,128)S(1)}, f32[128,1152]{1,0:T(8,128)S(1)}, u32[]{:S(2)}, u32[]{:S(2)}) collective-permute-start(f32[128,1152]{1,0:T(8,128)S(1)} %get-tuple-element.348), channel_id=1, source_target_pairs={{0,1},{1,2},{2,3},{3,4},{4,5},{5,6},{6,7},{7,8},{8,9},{9,10},{10,1... | collective-permute-start | bytes 1769480 | tf_op jit(solution)/shard_map/while/body/eval_jaxpr/ppermute | solution.py:12
  148.1 20.3 %collective-permute-start.1 = (f32[128,1152]{1,0:T(8,128)S(1)}, f32[128,1152]{1,0:T(8,128)S(1)}, u32[]{:S(2)}, u32[]{:S(2)}) collective-permute-start(f32[128,1152]{1,0:T(8,128)S(1)} %get-tuple-element.348), channel_id=1, source_target_pairs={{0,1},{1,2},{2,3},{3,4},{4,5},{5,6},{6,7},{7,8},{8,9},{9,10},{10,1... | collective-permute-start | bytes 1769480 | tf_op jit(solution)/shard_map/while/body/eval_jaxpr/ppermute | solution.py:12
  179.4 20.3 %collective-permute-start.1 = (f32[128,1152]{1,0:T(8,128)S(1)}, f32[128,1152]{1,0:T(8,128)S(1)}, u32[]{:S(2)}, u32[]{:S(2)}) collective-permute-start(f32[128,1152]{1,0:T(8,128)S(1)} %get-tuple-element.348), channel_id=1, source_target_pairs={{0,1},{1,2},{2,3},{3,4},{4,5},{5,6},{6,7},{7,8},{8,9},{9,10},{10,1... | collective-permute-start | bytes 1769480 | tf_op jit(solution)/shard_map/while/body/eval_jaxpr/ppermute | solution.py:12
  210.6 12.9 %collective-permute-start = (f32[128,1152]{1,0:T(8,128)S(1)}, f32[128,1152]{1,0:T(8,128)S(1)}, u32[]{:S(2)}, u32[]{:S(2)}) collective-permute-start(f32[128,1152]{1,0:T(8,128)S(1)} %get-tuple-element.347), channel_id=1, source_target_pairs={{0,1},{1,2},{2,3},{3,4},{4,5},{5,6},{6,7},{7,8},{8,9},{9,10},{10,1... | collective-permute-start | bytes 1769480 | tf_op jit(solution)/shard_map/while/body/eval_jaxpr/ppermute | solution.py:12
  210.6 20.3 %collective-permute-start.1 = (f32[128,1152]{1,0:T(8,128)S(1)}, f32[128,1152]{1,0:T(8,128)S(1)}, u32[]{:S(2)}, u32[]{:S(2)}) collective-permute-start(f32[128,1152]{1,0:T(8,128)S(1)} %get-tuple-element.348), channel_id=1, source_target_pairs={{0,1},{1,2},{2,3},{3,4},{4,5},{5,6},{6,7},{7,8},{8,9},{9,10},{10,1... | collective-permute-start | bytes 1769480 | tf_op jit(solution)/shard_map/while/body/eval_jaxpr/ppermute | solution.py:12
  241.9 20.3 %collective-permute-start.1 = (f32[128,1152]{1,0:T(8,128)S(1)}, f32[128,1152]{1,0:T(8,128)S(1)}, u32[]{:S(2)}, u32[]{:S(2)}) collective-permute-start(f32[128,1152]{1,0:T(8,128)S(1)} %get-tuple-element.348), channel_id=1, source_target_pairs={{0,1},{1,2},{2,3},{3,4},{4,5},{5,6},{6,7},{7,8},{8,9},{9,10},{10,1... | collective-permute-start | bytes 1769480 | tf_op jit(solution)/shard_map/while/body/eval_jaxpr/ppermute | solution.py:12
  273.2 12.9 %collective-permute-start = (f32[128,1152]{1,0:T(8,128)S(1)}, f32[128,1152]{1,0:T(8,128)S(1)}, u32[]{:S(2)}, u32[]{:S(2)}) collective-permute-start(f32[128,1152]{1,0:T(8,128)S(1)} %get-tuple-element.347), channel_id=1, source_target_pairs={{0,1},{1,2},{2,3},{3,4},{4,5},{5,6},{6,7},{7,8},{8,9},{9,10},{10,1... | collective-permute-start | bytes 1769480 | tf_op jit(solution)/shard_map/while/body/eval_jaxpr/ppermute | solution.py:12
  273.2 20.3 %collective-permute-start.1 = (f32[128,1152]{1,0:T(8,128)S(1)}, f32[128,1152]{1,0:T(8,128)S(1)}, u32[]{:S(2)}, u32[]{:S(2)}) collective-permute-start(f32[128,1152]{1,0:T(8,128)S(1)} %get-tuple-element.348), channel_id=1, source_target_pairs={{0,1},{1,2},{2,3},{3,4},{4,5},{5,6},{6,7},{7,8},{8,9},{9,10},{10,1... | collective-permute-start | bytes 1769480 | tf_op jit(solution)/shard_map/while/body/eval_jaxpr/ppermute | solution.py:12
  304.5 20.3 %collective-permute-start.1 = (f32[128,1152]{1,0:T(8,128)S(1)}, f32[128,1152]{1,0:T(8,128)S(1)}, u32[]{:S(2)}, u32[]{:S(2)}) collective-permute-start(f32[128,1152]{1,0:T(8,128)S(1)} %get-tuple-element.348), channel_id=1, source_target_pairs={{0,1},{1,2},{2,3},{3,4},{4,5},{5,6},{6,7},{7,8},{8,9},{9,10},{10,1... | collective-permute-start | bytes 1769480 | tf_op jit(solution)/shard_map/while/body/eval_jaxpr/ppermute | solution.py:12
  335.8 12.9 %collective-permute-start = (f32[128,1152]{1,0:T(8,128)S(1)}, f32[128,1152]{1,0:T(8,128)S(1)}, u32[]{:S(2)}, u32[]{:S(2)}) collective-permute-start(f32[128,1152]{1,0:T(8,128)S(1)} %get-tuple-element.347), channel_id=1, source_target_pairs={{0,1},{1,2},{2,3},{3,4},{4,5},{5,6},{6,7},{7,8},{8,9},{9,10},{10,1... | collective-permute-start | bytes 1769480 | tf_op jit(solution)/shard_map/while/body/eval_jaxpr/ppermute | solution.py:12
  335.8 20.3 %collective-permute-start.1 = (f32[128,1152]{1,0:T(8,128)S(1)}, f32[128,1152]{1,0:T(8,128)S(1)}, u32[]{:S(2)}, u32[]{:S(2)}) collective-permute-start(f32[128,1152]{1,0:T(8,128)S(1)} %get-tuple-element.348), channel_id=1, source_target_pairs={{0,1},{1,2},{2,3},{3,4},{4,5},{5,6},{6,7},{7,8},{8,9},{9,10},{10,1... | collective-permute-start | bytes 1769480 | tf_op jit(solution)/shard_map/while/body/eval_jaxpr/ppermute | solution.py:12
  367.1 20.3 %collective-permute-start.1 = (f32[128,1152]{1,0:T(8,128)S(1)}, f32[128,1152]{1,0:T(8,128)S(1)}, u32[]{:S(2)}, u32[]{:S(2)}) collective-permute-start(f32[128,1152]{1,0:T(8,128)S(1)} %get-tuple-element.348), channel_id=1, source_target_pairs={{0,1},{1,2},{2,3},{3,4},{4,5},{5,6},{6,7},{7,8},{8,9},{9,10},{10,1... | collective-permute-start | bytes 1769480 | tf_op jit(solution)/shard_map/while/body/eval_jaxpr/ppermute | solution.py:12
  398.3 12.9 %collective-permute-start = (f32[128,1152]{1,0:T(8,128)S(1)}, f32[128,1152]{1,0:T(8,128)S(1)}, u32[]{:S(2)}, u32[]{:S(2)}) collective-permute-start(f32[128,1152]{1,0:T(8,128)S(1)} %get-tuple-element.347), channel_id=1, source_target_pairs={{0,1},{1,2},{2,3},{3,4},{4,5},{5,6},{6,7},{7,8},{8,9},{9,10},{10,1... | collective-permute-start | bytes 1769480 | tf_op jit(solution)/shard_map/while/body/eval_jaxpr/ppermute | solution.py:12
  398.4 20.3 %collective-permute-start.1 = (f32[128,1152]{1,0:T(8,128)S(1)}, f32[128,1152]{1,0:T(8,128)S(1)}, u32[]{:S(2)}, u32[]{:S(2)}) collective-permute-start(f32[128,1152]{1,0:T(8,128)S(1)} %get-tuple-element.348), channel_id=1, source_target_pairs={{0,1},{1,2},{2,3},{3,4},{4,5},{5,6},{6,7},{7,8},{8,9},{9,10},{10,1... | collective-permute-start | bytes 1769480 | tf_op jit(solution)/shard_map/while/body/eval_jaxpr/ppermute | solution.py:12
  429.6 20.3 %collective-permute-start.1 = (f32[128,1152]{1,0:T(8,128)S(1)}, f32[128,1152]{1,0:T(8,128)S(1)}, u32[]{:S(2)}, u32[]{:S(2)}) collective-permute-start(f32[128,1152]{1,0:T(8,128)S(1)} %get-tuple-element.348), channel_id=1, source_target_pairs={{0,1},{1,2},{2,3},{3,4},{4,5},{5,6},{6,7},{7,8},{8,9},{9,10},{10,1... | collective-permute-start | bytes 1769480 | tf_op jit(solution)/shard_map/while/body/eval_jaxpr/ppermute | solution.py:12
  460.9 12.9 %collective-permute-start = (f32[128,1152]{1,0:T(8,128)S(1)}, f32[128,1152]{1,0:T(8,128)S(1)}, u32[]{:S(2)}, u32[]{:S(2)}) collective-permute-start(f32[128,1152]{1,0:T(8,128)S(1)} %get-tuple-element.347), channel_id=1, source_target_pairs={{0,1},{1,2},{2,3},{3,4},{4,5},{5,6},{6,7},{7,8},{8,9},{9,10},{10,1... | collective-permute-start | bytes 1769480 | tf_op jit(solution)/shard_map/while/body/eval_jaxpr/ppermute | solution.py:12
  460.9 20.3 %collective-permute-start.1 = (f32[128,1152]{1,0:T(8,128)S(1)}, f32[128,1152]{1,0:T(8,128)S(1)}, u32[]{:S(2)}, u32[]{:S(2)}) collective-permute-start(f32[128,1152]{1,0:T(8,128)S(1)} %get-tuple-element.348), channel_id=1, source_target_pairs={{0,1},{1,2},{2,3},{3,4},{4,5},{5,6},{6,7},{7,8},{8,9},{9,10},{10,1... | collective-permute-start | bytes 1769480 | tf_op jit(solution)/shard_map/while/body/eval_jaxpr/ppermute | solution.py:12
  492.2 20.3 %collective-permute-start.1 = (f32[128,1152]{1,0:T(8,128)S(1)}, f32[128,1152]{1,0:T(8,128)S(1)}, u32[]{:S(2)}, u32[]{:S(2)}) collective-permute-start(f32[128,1152]{1,0:T(8,128)S(1)} %get-tuple-element.348), channel_id=1, source_target_pairs={{0,1},{1,2},{2,3},{3,4},{4,5},{5,6},{6,7},{7,8},{8,9},{9,10},{10,1... | collective-permute-start | bytes 1769480 | tf_op jit(solution)/shard_map/while/body/eval_jaxpr/ppermute | solution.py:12
  523.5 20.3 %collective-permute-start.1 = (f32[128,1152]{1,0:T(8,128)S(1)}, f32[128,1152]{1,0:T(8,128)S(1)}, u32[]{:S(2)}, u32[]{:S(2)}) collective-permute-start(f32[128,1152]{1,0:T(8,128)S(1)} %get-tuple-element.348), channel_id=1, source_target_pairs={{0,1},{1,2},{2,3},{3,4},{4,5},{5,6},{6,7},{7,8},{8,9},{9,10},{10,1... | collective-permute-start | bytes 1769480 | tf_op jit(solution)/shard_map/while/body/eval_jaxpr/ppermute | solution.py:12
  554.8 13.0 %collective-permute-start.2 = (f32[128,1152]{1,0:T(8,128)S(1)}, f32[128,1152]{1,0:T(8,128)S(1)}, u32[]{:S(2)}, u32[]{:S(2)}) collective-permute-start(f32[128,1152]{1,0:T(8,128)S(1)} %get-tuple-element.249), channel_id=1, source_target_pairs={{0,1},{1,2},{2,3},{3,4},{4,5},{5,6},{6,7},{7,8},{8,9},{9,10},{10,1... | collective-permute-start | bytes 1769480 | tf_op jit(solution)/shard_map/ppermute | solution.py:12
  (74 other events, 855.1 us)
Sparse Core Ops, SparseCore 0:
  10.6 59.9 all-gather.1
  554.9 54.1 reduce-scatter.1
where the time goes:
time: 623 us; the launch traced here: 619 us
  waiting for transfers between devices  301 us (48%)
  matrix products  255 us (41%)
  local copies, waits for them, and re-layouts  33.4 us (5%)
  between operations  15.5 us (2%)
  other arithmetic  10.2 us (2%)
    ppermute x31, waiting for transfers between devices, from_behind(): return lax.ppermute(value, axis, pairs)  205 us
    dot_general x16, matrix products, pair_gradients(): lax.dot_general(photo_batch, sentence_tile, (((1,), (1,)), ((), ())), pre...  116 us
    dot_general x16, matrix products, pair_gradients(): jnp.dot(similarity_derivative, sentence_tile, precision=lax.Precision.HIG...  93.8 us
    all_gather x1, waiting for transfers between devices, per_device(): photo_batch = lax.all_gather(img_unit, 'row', axis=0, tiled=True)  56.3 us
    dot_general x16, matrix products, pair_gradients(): lax.dot_general(similarity_derivative, photo_batch, (((0,), (0,)), ((), (...  45.5 us
    reduce_scatter x1, waiting for transfers between devices, per_device(): lax.psum_scatter(group_sums, 'row', scatter_dimension=0, tiled=True)  40.1 us
    while x135, local copies, waits for them, and re-layouts  33.3 us
  transfers between devices with their start and end apart: 33, of which 18 were waited for; matrix products, arithmetic and copies ran while one was open for 18% of the time, Pallas kernels for 0%

commit v1 on v0

v1 whole, which is shorter than its diff:
```python
import functools

import jax
import jax.numpy as jnp
from jax import lax
from jax.experimental import pallas as pl
from jax.experimental.pallas import tpu as pltpu
from jax.sharding import Mesh
from jax.sharding import PartitionSpec as P

EPS = 1e-06
F32 = jnp.float32
BF16 = jnp.bfloat16
AXES = ("yl", "x", "yh", "z", "c")
PLACES = ((0, 0), (0, 1), (-1, 0), (1, 0), (-1, 1), (1, 1), (2, 0), (2, 1))


def shift_by(value, axis, steps):
    count = lax.axis_size(axis)
    return lax.ppermute(value, axis, [(i, (i + steps) % count) for i in range(count)])


def mm(a, b, ca, cb):
    return lax.dot_general(a, b, (((ca,), (cb,)), ((), ())), preferred_element_type=F32)


def halves(x):
    hi = x.astype(BF16)
    return hi, (x - hi.astype(F32)).astype(BF16)


def normalize_kernel(warmth, photo, text, photo_scaled, photo_unit, photo_len, text_unit, text_len):
    for raw, unit, length in ((photo, photo_unit, photo_len), (text, text_unit, text_len)):
        x = raw[...]
        size = jnp.sqrt(jnp.sum(x * x, axis=-1, keepdims=True) + EPS)
        unit[...] = x / size
        length[...] = size
    photo_scaled[...] = photo_unit[...] * jnp.exp(warmth[...])


def normalize(warmth, photo, text):
    n, d = photo.shape
    vm = pl.BlockSpec(memory_space=pltpu.VMEM)
    full = jax.ShapeDtypeStruct((n, d), F32)
    one = jax.ShapeDtypeStruct((n, 1), F32)
    return pl.pallas_call(
        normalize_kernel,
        in_specs=[vm, vm, vm],
        out_specs=[vm] * 5,
        out_shape=[full, full, one, full, one],
    )(warmth.reshape(1, 1), photo, text)


def pairs_kernel(bases, shift, img, match, txt, gi, gt, ah, al, bh, bl, *, ti, tj, n):
    j = pl.program_id(0)
    rows_all = img.shape[0]

    @pl.when(j == 0)
    def _():
        gi[...] = jnp.zeros_like(gi)

        def split(i, c):
            rows = pl.ds(pl.multiple_of(i * n, n), n)
            ah[rows, :], al[rows, :] = halves(img[rows, :])
            return c

        lax.fori_loop(0, rows_all // n, split, 0)

    bh[...], bl[...] = halves(txt[...])
    gt[...] = jnp.zeros_like(gt)
    lane = lax.broadcasted_iota(jnp.int32, (1, n), 1)
    per = tj // n
    col = jnp.concatenate([lane + bases[j * per + q] for q in range(per)], axis=1)

    def step(i, c):
        rows = pl.ds(pl.multiple_of(i * ti, ti), ti)
        a_h = ah[rows, :]
        a_l = al[rows, :]
        b_h = bh[...]
        b_l = bl[...]
        s = mm(a_h, b_h, 1, 1) + mm(a_h, b_l, 1, 1) + mm(a_l, b_h, 1, 1)
        p = 1.0 / (1.0 + jnp.exp(-(s + shift[0])))
        p = jnp.where(match[rows, :] == col, p - 1.0, p)
        p_h, p_l = halves(p)
        gi[rows, :] += mm(p_h, b_h, 1, 0) + mm(p_h, b_l, 1, 0) + mm(p_l, b_h, 1, 0)
        gt[...] += mm(p_h, a_h, 0, 0) + mm(p_h, a_l, 0, 0) + mm(p_l, a_h, 0, 0)
        return c

    lax.fori_loop(0, rows_all // ti, step, 0)


def pair_gradients(bases, shift, img, match, txt, n, ti=512, tj=512):
    rows, d = img.shape
    cols = txt.shape[0]
    sm = pl.BlockSpec(memory_space=pltpu.SMEM)
    return pl.pallas_call(
        functools.partial(pairs_kernel, ti=ti, tj=tj, n=n),
        grid=(cols // tj,),
        in_specs=[
            sm,
            sm,
            pl.BlockSpec((rows, d), lambda j: (0, 0)),
            pl.BlockSpec((rows, 1), lambda j: (0, 0)),
            pl.BlockSpec((tj, d), lambda j: (j, 0)),
        ],
        out_specs=[pl.BlockSpec((rows, d), lambda j: (0, 0)), pl.BlockSpec((tj, d), lambda j: (j, 0))],
        out_shape=[jax.ShapeDtypeStruct((rows, d), F32), jax.ShapeDtypeStruct((cols, d), F32)],
        scratch_shapes=[pltpu.VMEM((rows, d), BF16)] * 2 + [pltpu.VMEM((tj, d), BF16)] * 2,
        compiler_params=pltpu.CompilerParams(vmem_limit_bytes=58 * 2**20),
        cost_estimate=pl.CostEstimate(
            flops=18 * rows * cols * d, bytes_accessed=8 * (rows + cols) * d, transcendentals=2 * rows * cols
        ),
    )(bases, shift, img, match, txt)


def gather_shares(own, ring, pair):
    half = own.shape[0] // 2
    back = shift_by(own, ring, 1)
    front = shift_by(own, ring, -1)
    twin = shift_by(own, pair, 1)
    twin_back = shift_by(twin, ring, 1)
    twin_front = shift_by(twin, ring, -1)
    far = jnp.concatenate([shift_by(back[:half], ring, 1), shift_by(front[half:], ring, -1)])
    twin_far = jnp.concatenate([shift_by(twin_back[:half], ring, 1), shift_by(twin_front[half:], ring, -1)])
    return [own, twin, back, front, twin_back, twin_front, far, twin_far]


def reduce_shares(parts, ring, pair):
    own, twin, back, front, twin_back, twin_front, far, twin_far = parts
    half = own.shape[0] // 2

    def relay(ahead, behind, farthest):
        up = shift_by(farthest[:half], ring, 1)
        down = shift_by(farthest[half:], ring, -1)
        ahead = jnp.concatenate([ahead[:half] + up, ahead[half:]])
        behind = jnp.concatenate([behind[:half], behind[half:] + down])
        return shift_by(ahead, ring, 1) + shift_by(behind, ring, -1)

    twin = twin + relay(twin_front, twin_back, twin_far)
    return own + relay(front, back, far) + shift_by(twin, pair, 1)


def restore(grad, unit, length):
    along = jnp.sum(unit * grad, axis=-1, keepdims=True)
    return (grad - unit * along) / length


def per_device(photo, text, matching_index, warmth, shift):
    n = photo.shape[0]
    yl, x, yh, z, c = (lax.axis_index(a) for a in AXES)
    nx, nz = lax.axis_size("x"), lax.axis_size("z")
    ncol = lax.axis_size("yh") * nz * 2
    photo_scaled, photo_unit, photo_len, text_unit, text_len = normalize(warmth, photo, text)

    imgs = gather_shares(photo_scaled, "x", "yl")
    txts = []
    for share in gather_shares(text_unit, "z", "yh"):
        txts += [share, shift_by(share, "c", 1)]

    col = (yh * nz + z) * 2 + c
    rows = [(yl ^ dy) * nx + (x + dx) % nx for dx, dy in PLACES]
    match = jnp.concatenate([lax.dynamic_slice(matching_index, ((r * ncol + col) * n,), (n,)) for r in rows])
    row = yl * nx + x
    cols = [((yh ^ dy) * nz + (z + dz) % nz) * 2 + (c ^ k) for dz, dy in PLACES for k in (0, 1)]
    bases = jnp.stack([(row * ncol + q) * n for q in cols]).astype(jnp.int32)

    gi, gt = pair_gradients(bases, shift, jnp.concatenate(imgs), match[:, None], jnp.concatenate(txts), n)
    gi = [gi[k * n : (k + 1) * n] for k in range(8)]
    gt = [gt[k * n : (k + 1) * n] for k in range(16)]
    photo_grad = reduce_shares(gi, "x", "yl") * jnp.exp(warmth)
    text_grad = reduce_shares([gt[2 * k] + shift_by(gt[2 * k + 1], "c", 1) for k in range(8)], "z", "yh")
    return restore(photo_grad, photo_unit, photo_len), restore(text_grad, text_unit, text_len)


def solution(mesh):
    fine = Mesh(mesh.devices.reshape(2, 4, 2, 4, 2), AXES)
    spec = P(AXES, None)
    return jax.shard_map(
        per_device,
        mesh=fine,
        in_specs=(spec, spec, P(), P(), P()),
        out_specs=(spec, spec),
        check_vma=False,
    )
```

time: 623 us -> 263 us (0.42)
  matrix products: 255 us -> 0 us
  waiting for transfers between devices: 301 us -> 95.6 us
  Pallas kernels: 0 us -> 64.1 us
  starting transfers between devices: 1.96 us -> 56.8 us
  between operations: 15.5 us -> 2.37 us
    dot_general x48 -> x0, matrix products: 255 us -> none  [the longest x16 116 us: pair_gradients(): lax.dot_general(photo_batch, sentence_tile, (((1,), (1,)), ((), ())), pre...]
    ppermute x31 -> x52, waiting for transfers between devices: 205 us -> 95.6 us  [shift_by(): lax.ppermute(value, axis, [(i, (i + steps) % count) for i in range(count)])]
    pallas_call x0 -> x2, Pallas kernels: none -> 64.1 us  [the longest x1 61.4 us: pair_gradients(): pl.pallas_call(functools.partial(pairs_kernel, ti=ti, tj=tj, n=n), grid=(...]
    all_gather x1 -> x0, waiting for transfers between devices: 56.3 us -> none  [per_device(): photo_batch = lax.all_gather(img_unit, 'row', axis=0, tiled=True)]
    ppermute x31 -> x52, starting transfers between devices: 1.88 us -> 56.8 us  [shift_by(): lax.ppermute(value, axis, [(i, (i + steps) % count) for i in range(count)])]
    reduce_scatter x1 -> x0, waiting for transfers between devices: 40.1 us -> none  [per_device(): lax.psum_scatter(group_sums, 'row', scatter_dimension=0, tiled=True)]
    while x135 -> x0, local copies, waits for them, and re-layouts: 33.3 us -> none
    unnamed x10 -> x44, local copies, waits for them, and re-layouts: 0.02 us -> 27.7 us
  transfers between devices with their start and end apart: 33 -> 52, of which waited for: 18 -> 20; matrix products, arithmetic and copies ran while one was open for 18% -> 15% of each run, Pallas kernels for 0% -> 0%
where the time goes in v1:
time: 263 us; the launch traced here: 261 us
  waiting for transfers between devices  95.6 us (36%)
  Pallas kernels  64.1 us (24%)
  starting transfers between devices  56.8 us (22%)
  local copies, waits for them, and re-layouts  36.6 us (14%)
  other arithmetic  5.83 us (2%)
    ppermute x52, waiting for transfers between devices, shift_by(): lax.ppermute(value, axis, [(i, (i + steps) % count) for i in range(count)])  95.6 us
    pallas_call x1, Pallas kernels, pair_gradients(): pl.pallas_call(functools.partial(pairs_kernel, ti=ti, tj=tj, n=n), grid=(...  61.4 us
    ppermute x52, starting transfers between devices, shift_by(): lax.ppermute(value, axis, [(i, (i + steps) % count) for i in range(count)])  56.8 us
    unnamed x44, local copies, waits for them, and re-layouts  27.7 us
  transfers between devices with their start and end apart: 52, of which 20 were waited for; matrix products, arithmetic and copies ran while one was open for 15% of the time, Pallas kernels for 0%

profile of v1, /device:TPU:0, one launch (start us, length us, event | category | flops | bytes accessed | tf_op | source)
XLA Modules:
  0.0 261.3 jit_solution(39313237029811950)
XLA Ops:
  4.0 3.3 %collective-permute-start.10 = (f32[128,1152]{1,0:T(8,128)}, f32[128,1152]{1,0:T(8,128)S(1)}, u32[]{:S(2)}, u32[]{:S(2)}) collective-permute-start(f32[128,1152]{1,0:T(8,128)} %get-tuple-element.10), channel_id=1, source_target_pairs={{0,8},{8,0},{1,9},{9,1},{2,10},{10,2},{3,11},{11,3},{4,12},{12,4},... | collective-permute-start | bytes 1769480 | tf_op jit(solution)/shard_map/ppermute | solution.py:20
  20.5 4.7 %collective-permute-done.12 = f32[128,1152]{1,0:T(8,128)S(1)} collective-permute-done((f32[128,1152]{1,0:T(8,128)}, f32[128,1152]{1,0:T(8,128)S(1)}, u32[]{:S(2)}, u32[]{:S(2)}) %collective-permute-start.12) | collective-permute-done | bytes 589856 | tf_op jit(solution)/shard_map/ppermute | solution.py:20
  31.0 2.8 %collective-permute-start.2 = (f32[128,1152]{1,0:T(8,128)}, f32[128,1152]{1,0:T(8,128)S(1)}, u32[]{:S(2)}, u32[]{:S(2)}) collective-permute-start(f32[128,1152]{1,0:T(8,128)} %get-tuple-element.9), channel_id=1, source_target_pairs={{0,48},{16,0},{32,16},{48,32},{1,49},{17,1},{33,17},{49,33},{2,50}... | collective-permute-start | bytes 1769480 | tf_op jit(solution)/shard_map/ppermute | solution.py:20
  34.0 3.3 %collective-permute-start.21 = (f32[64,1152]{1,0:T(8,128)S(1)}, f32[64,1152]{1,0:T(8,128)S(1)}, u32[]{:S(2)}, u32[]{:S(2)}) collective-permute-start(f32[64,1152]{1,0:T(8,128)S(1)} %slice.223), channel_id=1, source_target_pairs={{0,6},{2,0},{4,2},{6,4},{1,7},{3,1},{5,3},{7,5},{8,14},{10,8},{12,... | collective-permute-start | bytes 884744 | tf_op jit(solution)/shard_map/ppermute | solution.py:20
  42.1 4.2 %collective-permute-done.2 = f32[128,1152]{1,0:T(8,128)S(1)} collective-permute-done((f32[128,1152]{1,0:T(8,128)}, f32[128,1152]{1,0:T(8,128)S(1)}, u32[]{:S(2)}, u32[]{:S(2)}) %collective-permute-start.2) | collective-permute-done | bytes 589856 | tf_op jit(solution)/shard_map/ppermute | solution.py:20
  47.8 3.3 %collective-permute-start.18 = (f32[128,1152]{1,0:T(8,128)S(1)}, f32[128,1152]{1,0:T(8,128)S(1)}, u32[]{:S(2)}, u32[]{:S(2)}) collective-permute-start(f32[128,1152]{1,0:T(8,128)S(1)} %collective-permute-done.10), channel_id=1, source_target_pairs={{0,6},{2,0},{4,2},{6,4},{1,7},{3,1},{5,3},{7,5},{8,14},{10,8},{12,... | collective-permute-start | bytes 1769480 | tf_op jit(solution)/shard_map/ppermute | solution.py:20
  59.0 5.2 %collective-permute-done.16 = f32[128,1152]{1,0:T(8,128)S(1)} collective-permute-done((f32[128,1152]{1,0:T(8,128)S(1)}, f32[128,1152]{1,0:T(8,128)S(1)}, u32[]{:S(2)}, u32[]{:S(2)}) %collective-permute-start.16) | collective-permute-done | bytes 589856 | tf_op jit(solution)/shard_map/ppermute | solution.py:20
  64.3 3.6 %collective-permute-start.6 = (f32[64,1152]{1,0:T(8,128)S(1)}, f32[64,1152]{1,0:T(8,128)S(1)}, u32[]{:S(2)}, u32[]{:S(2)}) collective-permute-start(f32[64,1152]{1,0:T(8,128)S(1)} %slice.219), channel_id=1, source_target_pairs={{0,48},{16,0},{32,16},{48,32},{1,49},{17,1},{33,17},{49,33},{2,50}... | collective-permute-start | bytes 884744 | tf_op jit(solution)/shard_map/ppermute | solution.py:20
  76.7 3.7 %collective-permute-start.8 = (f32[64,1152]{1,0:T(8,128)S(1)}, f32[64,1152]{1,0:T(8,128)S(1)}, u32[]{:S(2)}, u32[]{:S(2)}) collective-permute-start(f32[64,1152]{1,0:T(8,128)S(1)} %slice.221), channel_id=1, source_target_pairs={{0,48},{16,0},{32,16},{48,32},{1,49},{17,1},{33,17},{49,33},{2,50}... | collective-permute-start | bytes 884744 | tf_op jit(solution)/shard_map/ppermute | solution.py:20
  81.7 3.1 %collective-permute-done.7 = f32[64,1152]{1,0:T(8,128)S(1)} collective-permute-done((f32[64,1152]{1,0:T(8,128)S(1)}, f32[64,1152]{1,0:T(8,128)S(1)}, u32[]{:S(2)}, u32[]{:S(2)}) %collective-permute-start.7) | collective-permute-done | bytes 294944 | tf_op jit(solution)/shard_map/ppermute | solution.py:20
  93.7 61.4 %shard_map.69 = (f32[1024,1152]{1,0:T(8,128)}, f32[2048,1152]{1,0:T(8,128)}) custom-call(s32[16]{0:T(128)} %stack.67.bases, f32[1]{0:T(128)S(6)} %copy.43.shift, f32[1024,1152]{1,0:T(8,128)} %constant_dynamic-update-slice_fusion.img, s32[1024,1]{1,0:T(8,128)} %copy.7.match, f32[2048,1152]{1,0:T(8,128)} %constant_dynamic-update-slice_fusion.11.txt), custom_call_target="tpu_custom_call" | custom-call | flops 43486543872 | bytes 28311552 | tf_op jit(solution)/shard_map/pallas_call | solution.py:96
  157.6 3.1 %collective-permute-start.28 = (f32[64,1152]{1,0:T(8,128)S(1)}, f32[64,1152]{1,0:T(8,128)S(1)}, u32[]{:S(2)}, u32[]{:S(2)}) collective-permute-start(f32[64,1152]{1,0:T(8,128)S(1)} %get-tuple-element.39), channel_id=1, source_target_pairs={{0,48},{16,0},{32,16},{48,32},{1,49},{17,1},{33,17},{49,33},{2,50}... | collective-permute-start | bytes 884744 | tf_op jit(solution)/shard_map/ppermute | solution.py:20
  160.7 3.2 %collective-permute-start.32 = (f32[64,1152]{1,0:T(8,128)S(1)}, f32[64,1152]{1,0:T(8,128)S(1)}, u32[]{:S(2)}, u32[]{:S(2)}) collective-permute-start(f32[64,1152]{1,0:T(8,128)S(1)} %get-tuple-element.35), channel_id=1, source_target_pairs={{0,48},{16,0},{32,16},{48,32},{1,49},{17,1},{33,17},{49,33},{2,50}... | collective-permute-start | bytes 884744 | tf_op jit(solution)/shard_map/ppermute | solution.py:20
  163.9 2.8 %fusion = (f32[128,1152]{1,0:T(8,128)S(1)}, f32[128,1152]{1,0:T(8,128)S(1)}, f32[128,1152]{1,0:T(8,128)S(1)}, f32[128,1152]{1,0:T(8,128)S(1)}, f32[128,1152]{1,0...) fusion(f32[2048,1152]{1,0:T(8,128)} %get-tuple-element.14), kind=kLoop, calls=%fused_computation.68 | loop fusion | bytes 9437184 | tf_op jit(solution)/shard_map/slice | solution.py:169
  168.9 5.0 %collective-permute-done.30 = f32[64,1152]{1,0:T(8,128)S(1)} collective-permute-done((f32[64,1152]{1,0:T(8,128)S(1)}, f32[64,1152]{1,0:T(8,128)S(1)}, u32[]{:S(2)}, u32[]{:S(2)}) %collective-permute-start.30) | collective-permute-done | bytes 294944 | tf_op jit(solution)/shard_map/ppermute | solution.py:20
  178.1 3.2 %collective-permute-start.33 = (f32[128,1152]{1,0:T(8,128)S(1)}, f32[128,1152]{1,0:T(8,128)S(1)}, u32[]{:S(2)}, u32[]{:S(2)}) collective-permute-start(f32[128,1152]{1,0:T(8,128)S(1)} %pad_maximum_fusion.5), channel_id=1, source_target_pairs={{0,48},{16,0},{32,16},{48,32},{1,49},{17,1},{33,17},{49,33},{2,50}... | collective-permute-start | bytes 1769480 | tf_op jit(solution)/shard_map/ppermute | solution.py:20
  181.8 22.1 %collective-permute-done.33 = f32[128,1152]{1,0:T(8,128)S(1)} collective-permute-done((f32[128,1152]{1,0:T(8,128)S(1)}, f32[128,1152]{1,0:T(8,128)S(1)}, u32[]{:S(2)}, u32[]{:S(2)}) %collective-permute-start.33) | collective-permute-done | bytes 589856 | tf_op jit(solution)/shard_map/ppermute | solution.py:20
  204.2 3.1 %collective-permute-done.31 = f32[128,1152]{1,0:T(8,128)S(1)} collective-permute-done((f32[128,1152]{1,0:T(8,128)S(1)}, f32[128,1152]{1,0:T(8,128)S(1)}, u32[]{:S(2)}, u32[]{:S(2)}) %collective-permute-start.31) | collective-permute-done | bytes 589856 | tf_op jit(solution)/shard_map/ppermute | solution.py:20
  207.4 5.0 %collective-permute-done.41 = f32[64,1152]{1,0:T(8,128)S(1)} collective-permute-done((f32[64,1152]{1,0:T(8,128)S(1)}, f32[64,1152]{1,0:T(8,128)S(1)}, u32[]{:S(2)}, u32[]{:S(2)}) %collective-permute-start.41) | collective-permute-done | bytes 294944 | tf_op jit(solution)/shard_map/ppermute | solution.py:20
  214.0 6.1 %collective-permute-done.49 = f32[64,1152]{1,0:T(8,128)S(1)} collective-permute-done((f32[64,1152]{1,0:T(8,128)S(1)}, f32[64,1152]{1,0:T(8,128)S(1)}, u32[]{:S(2)}, u32[]{:S(2)}) %collective-permute-start.49) | collective-permute-done | bytes 294944 | tf_op jit(solution)/shard_map/ppermute | solution.py:20
  220.2 7.8 %collective-permute-done.46 = f32[64,1152]{1,0:T(8,128)S(1)} collective-permute-done((f32[64,1152]{1,0:T(8,128)S(1)}, f32[64,1152]{1,0:T(8,128)S(1)}, u32[]{:S(2)}, u32[]{:S(2)}) %collective-permute-start.46) | collective-permute-done | bytes 294944 | tf_op jit(solution)/shard_map/ppermute | solution.py:20
  231.9 8.1 %collective-permute-done.50 = f32[128,1152]{1,0:T(8,128)S(1)} collective-permute-done((f32[128,1152]{1,0:T(8,128)S(1)}, f32[128,1152]{1,0:T(8,128)S(1)}, u32[]{:S(2)}, u32[]{:S(2)}) %collective-permute-start.50) | collective-permute-done | bytes 589856 | tf_op jit(solution)/shard_map/ppermute | solution.py:20
  247.9 8.0 %collective-permute-done.42 = f32[128,1152]{1,0:T(8,128)S(1)} collective-permute-done((f32[128,1152]{1,0:T(8,128)S(1)}, f32[128,1152]{1,0:T(8,128)S(1)}, u32[]{:S(2)}, u32[]{:S(2)}) %collective-permute-start.42) | collective-permute-done | bytes 589856 | tf_op jit(solution)/shard_map/ppermute | solution.py:20
  256.0 3.6 %collective-permute-done.39 = f32[128,1152]{1,0:T(8,128)S(1)} collective-permute-done((f32[128,1152]{1,0:T(8,128)S(1)}, f32[128,1152]{1,0:T(8,128)S(1)}, u32[]{:S(2)}, u32[]{:S(2)}) %collective-permute-start.39) | collective-permute-done | bytes 589856 | tf_op jit(solution)/shard_map/ppermute | solution.py:20
  (169 shorter events, 79.0 us)
Async XLA Ops:
  4.0 30.0 %collective-permute-start.9 = (f32[128,1152]{1,0:T(8,128)}, f32[128,1152]{1,0:T(8,128)S(1)}, u32[]{:S(2)}, u32[]{:S(2)}) collective-permute-start(f32[128,1152]{1,0:T(8,128)} %get-tuple-element.10), channel_id=1, source_target_pairs={{0,1},{1,0},{2,3},{3,2},{4,5},{5,4},{6,7},{7,6},{8,9},{9,8},{10,11... | collective-permute-start | bytes 1769480 | tf_op jit(solution)/shard_map/ppermute | solution.py:20
  4.0 34.1 %collective-permute-start.10 = (f32[128,1152]{1,0:T(8,128)}, f32[128,1152]{1,0:T(8,128)S(1)}, u32[]{:S(2)}, u32[]{:S(2)}) collective-permute-start(f32[128,1152]{1,0:T(8,128)} %get-tuple-element.10), channel_id=1, source_target_pairs={{0,8},{8,0},{1,9},{9,1},{2,10},{10,2},{3,11},{11,3},{4,12},{12,4},... | collective-permute-start | bytes 1769480 | tf_op jit(solution)/shard_map/ppermute | solution.py:20
  7.3 18.0 %collective-permute-start.12 = (f32[128,1152]{1,0:T(8,128)}, f32[128,1152]{1,0:T(8,128)S(1)}, u32[]{:S(2)}, u32[]{:S(2)}) collective-permute-start(f32[128,1152]{1,0:T(8,128)} %get-tuple-element.10), channel_id=1, source_target_pairs={{0,2},{2,4},{4,6},{6,0},{1,3},{3,5},{5,7},{7,1},{8,10},{10,12},{12... | collective-permute-start | bytes 1769480 | tf_op jit(solution)/shard_map/ppermute | solution.py:20
  9.2 21.8 %collective-permute-start.14 = (f32[128,1152]{1,0:T(8,128)}, f32[128,1152]{1,0:T(8,128)S(1)}, u32[]{:S(2)}, u32[]{:S(2)}) collective-permute-start(f32[128,1152]{1,0:T(8,128)} %get-tuple-element.10), channel_id=1, source_target_pairs={{0,6},{2,0},{4,2},{6,4},{1,7},{3,1},{5,3},{7,5},{8,14},{10,8},{12,... | collective-permute-start | bytes 1769480 | tf_op jit(solution)/shard_map/ppermute | solution.py:20
  11.3 22.6 %collective-permute-start.1 = (f32[128,1152]{1,0:T(8,128)}, f32[128,1152]{1,0:T(8,128)S(1)}, u32[]{:S(2)}, u32[]{:S(2)}) collective-permute-start(f32[128,1152]{1,0:T(8,128)} %get-tuple-element.9), channel_id=1, source_target_pairs={{0,16},{16,32},{32,48},{48,0},{1,17},{17,33},{33,49},{49,1},{2,18}... | collective-permute-start | bytes 1769480 | tf_op jit(solution)/shard_map/ppermute | solution.py:20
  25.3 15.2 %collective-permute-start = (f32[128,1152]{1,0:T(8,128)}, f32[128,1152]{1,0:T(8,128)S(1)}, u32[]{:S(2)}, u32[]{:S(2)}) collective-permute-start(f32[128,1152]{1,0:T(8,128)} %get-tuple-element.9), channel_id=1, source_target_pairs={{0,64},{64,0},{1,65},{65,1},{2,66},{66,2},{3,67},{67,3},{4,68},{68... | collective-permute-start | bytes 1769480 | tf_op jit(solution)/shard_map/ppermute | solution.py:20
  31.0 15.3 %collective-permute-start.2 = (f32[128,1152]{1,0:T(8,128)}, f32[128,1152]{1,0:T(8,128)S(1)}, u32[]{:S(2)}, u32[]{:S(2)}) collective-permute-start(f32[128,1152]{1,0:T(8,128)} %get-tuple-element.9), channel_id=1, source_target_pairs={{0,48},{16,0},{32,16},{48,32},{1,49},{17,1},{33,17},{49,33},{2,50}... | collective-permute-start | bytes 1769480 | tf_op jit(solution)/shard_map/ppermute | solution.py:20
  33.9 13.4 %collective-permute-start.20 = (f32[64,1152]{1,0:T(8,128)S(1)}, f32[64,1152]{1,0:T(8,128)S(1)}, u32[]{:S(2)}, u32[]{:S(2)}) collective-permute-start(f32[64,1152]{1,0:T(8,128)S(1)} %slice.222), channel_id=1, source_target_pairs={{0,2},{2,4},{4,6},{6,0},{1,3},{3,5},{5,7},{7,1},{8,10},{10,12},{12... | collective-permute-start | bytes 884744 | tf_op jit(solution)/shard_map/ppermute | solution.py:20
  34.0 13.8 %collective-permute-start.21 = (f32[64,1152]{1,0:T(8,128)S(1)}, f32[64,1152]{1,0:T(8,128)S(1)}, u32[]{:S(2)}, u32[]{:S(2)}) collective-permute-start(f32[64,1152]{1,0:T(8,128)S(1)} %slice.223), channel_id=1, source_target_pairs={{0,6},{2,0},{4,2},{6,4},{1,7},{3,1},{5,3},{7,5},{8,14},{10,8},{12,... | collective-permute-start | bytes 884744 | tf_op jit(solution)/shard_map/ppermute | solution.py:20
  38.1 36.5 %collective-permute-start.5 = (f32[64,1152]{1,0:T(8,128)S(1)}, f32[64,1152]{1,0:T(8,128)S(1)}, u32[]{:S(2)}, u32[]{:S(2)}) collective-permute-start(f32[64,1152]{1,0:T(8,128)S(1)} %slice.218), channel_id=1, source_target_pairs={{0,16},{16,32},{32,48},{48,0},{1,17},{17,33},{33,49},{49,1},{2,18}... | collective-permute-start | bytes 884744 | tf_op jit(solution)/shard_map/ppermute | solution.py:20
  47.7 16.5 %collective-permute-start.16 = (f32[128,1152]{1,0:T(8,128)S(1)}, f32[128,1152]{1,0:T(8,128)S(1)}, u32[]{:S(2)}, u32[]{:S(2)}) collective-permute-start(f32[128,1152]{1,0:T(8,128)S(1)} %collective-permute-done.10), channel_id=1, source_target_pairs={{0,2},{2,4},{4,6},{6,0},{1,3},{3,5},{5,7},{7,1},{8,10},{10,12},{12... | collective-permute-start | bytes 1769480 | tf_op jit(solution)/shard_map/ppermute | solution.py:20
  47.8 22.5 %collective-permute-start.18 = (f32[128,1152]{1,0:T(8,128)S(1)}, f32[128,1152]{1,0:T(8,128)S(1)}, u32[]{:S(2)}, u32[]{:S(2)}) collective-permute-start(f32[128,1152]{1,0:T(8,128)S(1)} %collective-permute-done.10), channel_id=1, source_target_pairs={{0,6},{2,0},{4,2},{6,4},{1,7},{3,1},{5,3},{7,5},{8,14},{10,8},{12,... | collective-permute-start | bytes 1769480 | tf_op jit(solution)/shard_map/ppermute | solution.py:20
  52.8 16.6 %collective-permute-start.3 = (f32[128,1152]{1,0:T(8,128)S(1)}, f32[128,1152]{1,0:T(8,128)S(1)}, u32[]{:S(2)}, u32[]{:S(2)}) collective-permute-start(f32[128,1152]{1,0:T(8,128)S(1)} %collective-permute-done), channel_id=1, source_target_pairs={{0,16},{16,32},{32,48},{48,0},{1,17},{17,33},{33,49},{49,1},{2,18}... | collective-permute-start | bytes 1769480 | tf_op jit(solution)/shard_map/ppermute | solution.py:20
  55.7 16.3 %collective-permute-start.4 = (f32[128,1152]{1,0:T(8,128)S(1)}, f32[128,1152]{1,0:T(8,128)S(1)}, u32[]{:S(2)}, u32[]{:S(2)}) collective-permute-start(f32[128,1152]{1,0:T(8,128)S(1)} %collective-permute-done), channel_id=1, source_target_pairs={{0,48},{16,0},{32,16},{48,32},{1,49},{17,1},{33,17},{49,33},{2,50}... | collective-permute-start | bytes 1769480 | tf_op jit(solution)/shard_map/ppermute | solution.py:20
  69.4 21.0 %collective-permute-start.22 = (f32[128,1152]{1,0:T(8,128)S(1)}, f32[128,1152]{1,0:T(8,128)S(1)}, u32[]{:S(2)}, u32[]{:S(2)}) collective-permute-start(f32[128,1152]{1,0:T(8,128)S(1)} %pad_maximum_fusion), channel_id=1, source_target_pairs={{0,1},{1,0},{2,3},{3,2},{4,5},{5,4},{6,7},{7,6},{8,9},{9,8},{10,11... | collective-permute-start | bytes 1769480 | tf_op jit(solution)/shard_map/ppermute | solution.py:20
  175.0 55.3 %collective-permute-start.43 = (f32[128,1152]{1,0:T(8,128)S(1)}, f32[128,1152]{1,0:T(8,128)S(1)}, u32[]{:S(2)}, u32[]{:S(2)}) collective-permute-start(f32[128,1152]{1,0:T(8,128)S(1)} %get-tuple-element.24), channel_id=1, source_target_pairs={{0,1},{1,0},{2,3},{3,2},{4,5},{5,4},{6,7},{7,6},{8,9},{9,8},{10,11... | collective-permute-start | bytes 1769480 | tf_op jit(solution)/shard_map/ppermute | solution.py:20
  175.6 67.3 %collective-permute-start.29 = (f32[128,1152]{1,0:T(8,128)S(1)}, f32[128,1152]{1,0:T(8,128)S(1)}, u32[]{:S(2)}, u32[]{:S(2)}) collective-permute-start(f32[128,1152]{1,0:T(8,128)S(1)} %pad_maximum_fusion.3), channel_id=1, source_target_pairs={{0,48},{16,0},{32,16},{48,32},{1,49},{17,1},{33,17},{49,33},{2,50}... | collective-permute-start | bytes 1769480 | tf_op jit(solution)/shard_map/ppermute | solution.py:20
  178.1 66.7 %collective-permute-start.27 = (f32[128,1152]{1,0:T(8,128)S(1)}, f32[128,1152]{1,0:T(8,128)S(1)}, u32[]{:S(2)}, u32[]{:S(2)}) collective-permute-start(f32[128,1152]{1,0:T(8,128)S(1)} %pad_maximum_fusion.2), channel_id=1, source_target_pairs={{0,16},{16,32},{32,48},{48,0},{1,17},{17,33},{33,49},{49,1},{2,18}... | collective-permute-start | bytes 1769480 | tf_op jit(solution)/shard_map/ppermute | solution.py:20
  178.1 25.8 %collective-permute-start.33 = (f32[128,1152]{1,0:T(8,128)S(1)}, f32[128,1152]{1,0:T(8,128)S(1)}, u32[]{:S(2)}, u32[]{:S(2)}) collective-permute-start(f32[128,1152]{1,0:T(8,128)S(1)} %pad_maximum_fusion.5), channel_id=1, source_target_pairs={{0,48},{16,0},{32,16},{48,32},{1,49},{17,1},{33,17},{49,33},{2,50}... | collective-permute-start | bytes 1769480 | tf_op jit(solution)/shard_map/ppermute | solution.py:20
  181.3 26.0 %collective-permute-start.31 = (f32[128,1152]{1,0:T(8,128)S(1)}, f32[128,1152]{1,0:T(8,128)S(1)}, u32[]{:S(2)}, u32[]{:S(2)}) collective-permute-start(f32[128,1152]{1,0:T(8,128)S(1)} %pad_maximum_fusion.4), channel_id=1, source_target_pairs={{0,16},{16,32},{32,48},{48,0},{1,17},{17,33},{33,49},{49,1},{2,18}... | collective-permute-start | bytes 1769480 | tf_op jit(solution)/shard_map/ppermute | solution.py:20
  207.3 22.9 %collective-permute-start.38 = (f32[64,1152]{1,0:T(8,128)S(1)}, f32[64,1152]{1,0:T(8,128)S(1)}, u32[]{:S(2)}, u32[]{:S(2)}) collective-permute-start(f32[64,1152]{1,0:T(8,128)S(1)} %get-tuple-element.49), channel_id=1, source_target_pairs={{0,2},{2,4},{4,6},{6,0},{1,3},{3,5},{5,7},{7,1},{8,10},{10,12},{12... | collective-permute-start | bytes 884744 | tf_op jit(solution)/shard_map/ppermute | solution.py:20
  230.4 16.3 %collective-permute-start.34 = (f32[128,1152]{1,0:T(8,128)S(1)}, f32[128,1152]{1,0:T(8,128)S(1)}, u32[]{:S(2)}, u32[]{:S(2)}) collective-permute-start(f32[128,1152]{1,0:T(8,128)S(1)} %add_add_fusion.2), channel_id=1, source_target_pairs={{0,64},{64,0},{1,65},{65,1},{2,66},{66,2},{3,67},{67,3},{4,68},{68... | collective-permute-start | bytes 1769480 | tf_op jit(solution)/shard_map/ppermute | solution.py:20
  242.8 16.7 %collective-permute-start.39 = (f32[128,1152]{1,0:T(8,128)S(1)}, f32[128,1152]{1,0:T(8,128)S(1)}, u32[]{:S(2)}, u32[]{:S(2)}) collective-permute-start(f32[128,1152]{1,0:T(8,128)S(1)} %pad_maximum_fusion.6), channel_id=1, source_target_pairs={{0,2},{2,4},{4,6},{6,0},{1,3},{3,5},{5,7},{7,1},{8,10},{10,12},{12... | collective-permute-start | bytes 1769480 | tf_op jit(solution)/shard_map/ppermute | solution.py:20
  244.8 15.1 %collective-permute-start.51 = (f32[128,1152]{1,0:T(8,128)S(1)}, f32[128,1152]{1,0:T(8,128)S(1)}, u32[]{:S(2)}, u32[]{:S(2)}) collective-permute-start(f32[128,1152]{1,0:T(8,128)S(1)} %add_add_fusion), channel_id=1, source_target_pairs={{0,8},{8,0},{1,9},{9,1},{2,10},{10,2},{3,11},{11,3},{4,12},{12,4},... | collective-permute-start | bytes 1769480 | tf_op jit(solution)/shard_map/ppermute | solution.py:20
  (34 other events, 428.7 us)

commit v2 on v1

v2 whole, which is shorter than its diff:
```python
import functools

import jax
import jax.numpy as jnp
from jax import lax
from jax.experimental import pallas as pl
from jax.experimental.pallas import tpu as pltpu
from jax.sharding import Mesh
from jax.sharding import PartitionSpec as P

EPS = 1e-06
F32 = jnp.float32
BF16 = jnp.bfloat16
AXES = ("yl", "x", "yh", "z", "c")
PLACES = ((0, 0), (0, 1), (-1, 0), (1, 1), (2, 0), (2, 1), (1, 0), (-1, 1))


def shift_by(value, axis, steps):
    count = lax.axis_size(axis)
    return lax.ppermute(value, axis, [(i, (i + steps) % count) for i in range(count)])


def mm(a, b, ca, cb):
    return lax.dot_general(a, b, (((ca,), (cb,)), ((), ())), preferred_element_type=F32)


def halves(x):
    hi = x.astype(BF16)
    return hi, (x - hi.astype(F32)).astype(BF16)


def normalize_kernel(warmth, photo, text, photo_scaled, photo_unit, photo_len, text_unit, text_len):
    for raw, unit, length in ((photo, photo_unit, photo_len), (text, text_unit, text_len)):
        x = raw[...]
        size = jnp.sqrt(jnp.sum(x * x, axis=-1, keepdims=True) + EPS)
        unit[...] = x / size
        length[...] = size
    photo_scaled[...] = photo_unit[...] * jnp.exp(warmth[...])


def normalize(warmth, photo, text):
    n, d = photo.shape
    vm = pl.BlockSpec(memory_space=pltpu.VMEM)
    full = jax.ShapeDtypeStruct((n, d), F32)
    one = jax.ShapeDtypeStruct((n, 1), F32)
    return pl.pallas_call(
        normalize_kernel,
        in_specs=[vm, vm, vm],
        out_specs=[vm] * 5,
        out_shape=[full, full, one, full, one],
    )(warmth.reshape(1, 1), photo, text)


def pairs_kernel(bases, shift, match, *refs, shares, parts, n, ti, tj):
    imgs, refs = refs[:shares], refs[shares:]
    count = sum(len(p) for p in parts)
    txts, gi_out, gt_out = refs[:count], refs[count : count + shares], refs[count + shares : 2 * count + shares]
    gi, gt, raw, ah, al, bh, bl, img_in, img_out, txt_in, txt_out = refs[2 * count + shares :]
    j = pl.program_id(0)
    last = len(parts) - 1

    def text_copies(k, refs, buf, sems, out):
        row, copies = 0, []
        for i, q in enumerate(parts[k]):
            here = buf.at[k % 2, pl.ds(row, q[1])]
            there = refs[q[0]]
            sem = sems.at[k % 2, i]
            copies.append(pltpu.make_async_copy(here, there, sem) if out else pltpu.make_async_copy(there, here, sem))
            row += q[1]
        return copies

    def text_in(k):
        return text_copies(k, txts, raw, txt_in, False)

    def text_out(k):
        return text_copies(k, gt_out, gt, txt_out, True)

    @pl.when(j == 0)
    def _():
        copies = [pltpu.make_async_copy(imgs[k], gi.at[pl.ds(k * n, n)], img_in.at[k]) for k in range(shares)]
        for c in copies + text_in(0):
            c.start()
        for k, c in enumerate(copies):
            c.wait()
            rows = pl.ds(k * n, n)
            ah[rows, :], al[rows, :] = halves(gi[rows, :])
        gi[...] = jnp.zeros_like(gi)

    for k in range(last + 1):

        @pl.when(j == k)
        def _():
            if k < last:
                for c in text_in(k + 1):
                    c.start()
            for c in text_in(k):
                c.wait()
            if k >= 2:
                for c in text_out(k - 2):
                    c.wait()

    slot = j % 2
    bh[...], bl[...] = halves(raw[slot])
    gt[slot] = jnp.zeros((tj, gt.shape[2]), F32)
    lane = lax.broadcasted_iota(jnp.int32, (1, n), 1)
    per = tj // n
    col = jnp.concatenate([lane + bases[j * per + q] for q in range(per)], axis=1)

    def step(i, c):
        rows = pl.ds(pl.multiple_of(i * ti, ti), ti)
        a_h = ah[rows, :]
        a_l = al[rows, :]
        b_h = bh[...]
        b_l = bl[...]
        s = mm(a_h, b_h, 1, 1) + mm(a_h, b_l, 1, 1) + mm(a_l, b_h, 1, 1)
        p = 1.0 / (1.0 + jnp.exp(-(s + shift[0])))
        p = jnp.where(match[rows, :] == col, p - 1.0, p)
        p_h, p_l = halves(p)
        gi[rows, :] += mm(p_h, b_h, 1, 0) + mm(p_h, b_l, 1, 0) + mm(p_l, b_h, 1, 0)
        gt[slot] += mm(p_h, a_h, 0, 0) + mm(p_h, a_l, 0, 0) + mm(p_l, a_h, 0, 0)
        return c

    lax.fori_loop(0, shares * n // ti, step, 0)

    for k in range(last + 1):

        @pl.when(j == k)
        def _():
            for c in text_out(k):
                c.start()

    @pl.when(j == last)
    def _():
        copies = [pltpu.make_async_copy(gi.at[pl.ds(k * n, n)], gi_out[k], img_out.at[k]) for k in range(shares)]
        for c in copies:
            c.start()
        for c in copies + text_out(last - 1) + text_out(last):
            c.wait()


def pair_gradients(shift, imgs, match, txts, parts, bases, ti=512):
    n, d = imgs[0].shape
    rows, tj = len(imgs) * n, sum(q[1] for q in parts[0])
    cols = len(parts) * tj
    sm, vm, far = (pl.BlockSpec(memory_space=m) for m in (pltpu.SMEM, pltpu.VMEM, pl.ANY))
    out = [jax.ShapeDtypeStruct(x.shape, F32) for x in (*imgs, *txts)]
    out = pl.pallas_call(
        functools.partial(pairs_kernel, shares=len(imgs), parts=parts, n=n, ti=ti, tj=tj),
        grid=(len(parts),),
        in_specs=[sm, sm, vm] + [far] * len(out),
        out_specs=[far] * len(out),
        scratch_shapes=[pltpu.VMEM((rows, d), F32)]
        + [pltpu.VMEM((2, tj, d), F32)] * 2
        + [pltpu.VMEM((rows, d), BF16)] * 2
        + [pltpu.VMEM((tj, d), BF16)] * 2
        + [pltpu.SemaphoreType.DMA((len(imgs),))] * 2
        + [pltpu.SemaphoreType.DMA((2, 2))] * 2,
        out_shape=out,
        compiler_params=pltpu.CompilerParams(vmem_limit_bytes=58 * 2**20),
        cost_estimate=pl.CostEstimate(
            flops=18 * rows * cols * d, bytes_accessed=8 * (rows + cols) * d, transcendentals=2 * rows * cols
        ),
    )(bases, shift, match, *imgs, *txts)
    return out[: len(imgs)], out[len(imgs) :]


def gather_shares(photo, text):
    hold = lax.optimization_barrier
    ups, downs = [(photo, text)], []
    up, down = hold(
        (
            (shift_by(photo, "x", 1), shift_by(text, "z", 1)),
            (shift_by(photo, "yl", 1), shift_by(text, "yh", 1)),
        )
    )
    for hop in range(3):
        ups.append(up)
        downs.append(down)
        nxt = tuple(shift_by(v, a, -1) for v, a in zip(down, ("x", "z")))
        if hop < 2:
            up, down = hold((tuple(shift_by(v, a, 1) for v, a in zip(up, ("x", "z"))), nxt))
        else:
            downs.append(hold(nxt))
    return ([pair[k] for both in zip(ups, downs) for pair in both] for k in (0, 1))


def reduce_shares(photo, text_mine, text_other):
    hold = lax.optimization_barrier
    i_own, i_twin, i_back, i_twin_front, i_far, i_twin_far, i_front, i_twin_back = photo
    n = i_own.shape[0]

    def join(k, other):
        both = text_mine[k] + shift_by(other, "c", 1)
        return both[:n], both[n:]

    i_up, i_down = shift_by(i_far, "x", 1), shift_by(i_twin_far, "x", -1)
    t_far, t_twin_far = join(2, text_other[2])
    rest = (text_other[0], text_other[1], text_other[3])
    rest, t_far, t_twin_far = hold((rest, t_far, t_twin_far))
    t_up, t_down = shift_by(t_far, "z", 1), shift_by(t_twin_far, "z", -1)
    i_up, i_down, t_up, t_down = hold((i_up, i_down, t_up, t_down))
    t_back, t_twin_front = join(1, rest[1])
    t_front, t_twin_back = join(3, rest[2])
    i_p, i_q = shift_by(i_twin_front, "x", 1), shift_by(i_twin_back + i_down, "x", -1)
    near, t_up, t_down = hold((rest[0], t_up, t_down))
    t_own, t_twin = join(0, near)
    t_p, t_q = shift_by(t_twin_front, "z", 1), shift_by(t_twin_back + t_down, "z", -1)
    i_back, t_back, i_p, i_q = hold((i_back, t_back, i_p, i_q))
    i_y = shift_by(i_twin + i_p + i_q, "yl", 1)
    i_r, i_s = shift_by(i_front + i_up, "x", 1), shift_by(i_back, "x", -1)
    t_s = shift_by(t_back, "z", -1)
    t_front, t_p = hold((t_front + t_up, t_p))
    t_y = shift_by(t_twin + t_p + t_q, "yh", 1)
    t_r = shift_by(t_front, "z", 1)
    return i_own + i_r + i_s + i_y, t_own + t_r + t_s + t_y


def restore(grad, unit, length):
    along = jnp.sum(unit * grad, axis=-1, keepdims=True)
    return (grad - unit * along) / length


def per_device(photo, text, matching_index, warmth, shift):
    n = photo.shape[0]
    yl, x, yh, z, c = (lax.axis_index(a) for a in AXES)
    nx, nz = lax.axis_size("x"), lax.axis_size("z")
    ncol = lax.axis_size("yh") * nz * 2
    photo_scaled, photo_unit, photo_len, text_unit, text_len = normalize(warmth, photo, text)

    imgs, txts = gather_shares(photo_scaled, text_unit)
    txts = [jnp.concatenate(txts[k : k + 2]) for k in range(0, 8, 2)]
    txts = [t for own in txts for t in (own, shift_by(own, "c", 1))]
    parts = [((2 * k, 2 * n), (2 * k + 1, 2 * n)) for k in range(4)]

    col = (yh * nz + z) * 2 + c
    row = yl * nx + x
    places = [(yl ^ dy) * nx + (x + dx) % nx for dx, dy in PLACES]
    match = jnp.concatenate([lax.dynamic_slice(matching_index, ((r * ncol + col) * n,), (n,)) for r in places])
    match = match[:, None]
    mine, other = ([((yh ^ dy) * nz + (z + dz) % nz) * 2 + (c ^ k) for dz, dy in PLACES] for k in (0, 1))
    cols = [q for k in range(0, 8, 2) for q in mine[k : k + 2] + other[k : k + 2]]
    bases = jnp.stack([(row * ncol + q) * n for q in cols]).astype(jnp.int32)

    gi, gt = pair_gradients(shift, imgs, match, txts, parts, bases)
    photo_grad, text_grad = reduce_shares(gi, gt[0::2], gt[1::2])
    photo_grad = photo_grad * jnp.exp(warmth)
    return restore(photo_grad, photo_unit, photo_len), restore(text_grad, text_unit, text_len)


def solution(mesh):
    fine = Mesh(mesh.devices.reshape(2, 4, 2, 4, 2), AXES)
    spec = P(AXES, None)
    return jax.shard_map(
        per_device,
        mesh=fine,
        in_specs=(spec, spec, P(), P(), P()),
        out_specs=(spec, spec),
        check_vma=False,
    )
```

time: 263 us -> 234 us (0.89)
  local copies, waits for them, and re-layouts: 36.6 us -> 13.3 us
  starting transfers between devices: 56.8 us -> 45.1 us
  other arithmetic: 5.83 us -> 10.1 us
    unnamed x44 -> x61, local copies, waits for them, and re-layouts: 27.7 us -> 8.89 us
    ppermute x52 -> x36, starting transfers between devices: 56.8 us -> 45.1 us  [shift_by(): lax.ppermute(value, axis, [(i, (i + steps) % count) for i in range(count)])]
    slice x12 -> x2, local copies, waits for them, and re-layouts: 4.91 us -> 0.97 us  [join(): return (both[:n], both[n:])]
    add x6 -> x9, other arithmetic: 0.84 us -> 3.99 us  [the longest x4 1.9 us: join(): both = text_mine[k] + shift_by(other, 'c', 1)]
    ppermute x52 -> x36, waiting for transfers between devices: 95.6 us -> 98.1 us  [shift_by(): lax.ppermute(value, axis, [(i, (i + steps) % count) for i in range(count)])]
  transfers between devices with their start and end apart: 52 -> 36, of which waited for: 20 -> 22; matrix products, arithmetic and copies ran while one was open for 15% -> 8% of each run, Pallas kernels for 0% -> 0%
where the time goes in v2:
time: 234 us; the launch traced here: 233 us
  waiting for transfers between devices  98.1 us (42%)
  Pallas kernels  64.3 us (27%)
  starting transfers between devices  45.1 us (19%)
  local copies, waits for them, and re-layouts  13.3 us (6%)
  other arithmetic  10.1 us (4%)
  between operations  2.61 us (1%)
    ppermute x36, waiting for transfers between devices, shift_by(): lax.ppermute(value, axis, [(i, (i + steps) % count) for i in range(count)])  98.1 us
    pallas_call x1, Pallas kernels, pair_gradients(): pl.pallas_call(functools.partial(pairs_kernel, shares=len(imgs), parts=pa...  61.6 us
    ppermute x36, starting transfers between devices, shift_by(): lax.ppermute(value, axis, [(i, (i + steps) % count) for i in range(count)])  45.1 us
    unnamed x61, local copies, waits for them, and re-layouts  8.89 us
  transfers between devices with their start and end apart: 36, of which 22 were waited for; matrix products, arithmetic and copies ran while one was open for 8% of the time, Pallas kernels for 0%

profile of v2, /device:TPU:0, one launch (start us, length us, event | category | flops | bytes accessed | tf_op | source)
XLA Modules:
  0.0 233.5 jit_solution(17772540668238128588)
XLA Ops:
  1.3 2.7 %shard_map.68 = (f32[128,1152]{1,0:T(8,128)}, f32[128,1152]{1,0:T(8,128)}, f32[128,1]{1,0:T(8,128)}, f32[128,1152]{1,0:T(8,128)}, f32[128,1]{1,0:T(8,128)}) custom-call(f32[1,1]{1,0:T(1,128)} %bitcast.19.warmth, f32[128,1152]{1,0:T(8,128)} %photo.1, f32[128,1152]{1,0:T(8,128)} %text.1), custom_call_target="tpu_custom_call" | custom-call | tf_op jit(solution)/shard_map/pallas_call | solution.py:46
  7.1 2.9 %collective-permute-start.3 = (f32[128,1152]{1,0:T(8,128)}, f32[128,1152]{1,0:T(8,128)S(1)}, u32[]{:S(2)}, u32[]{:S(2)}) collective-permute-start(f32[128,1152]{1,0:T(8,128)} %get-tuple-element.56), channel_id=1, source_target_pairs={{0,8},{8,0},{1,9},{9,1},{2,10},{10,2},{3,11},{11,3},{4,12},{12,4},... | collective-permute-start | bytes 1769480 | tf_op jit(solution)/shard_map/ppermute | solution.py:20
  11.9 8.5 %collective-permute-done.2.refs_1_ = f32[128,1152]{1,0:T(8,128)S(1)} collective-permute-done((f32[128,1152]{1,0:T(8,128)}, f32[128,1152]{1,0:T(8,128)S(1)}, u32[]{:S(2)}, u32[]{:S(2)}) %collective-permute-start.2) | collective-permute-done | bytes 589856 | tf_op jit(solution)/shard_map/ppermute | solution.py:20
  21.8 12.6 %collective-permute-done.3 = f32[128,1152]{1,0:T(8,128)S(1)} collective-permute-done((f32[128,1152]{1,0:T(8,128)}, f32[128,1152]{1,0:T(8,128)S(1)}, u32[]{:S(2)}, u32[]{:S(2)}) %collective-permute-start.3) | collective-permute-done | bytes 589856 | tf_op jit(solution)/shard_map/ppermute | solution.py:20
  34.4 2.8 %collective-permute-start.6 = (f32[128,1152]{1,0:T(8,128)S(1)}, f32[128,1152]{1,0:T(8,128)S(1)}, u32[]{:S(2)}, u32[]{:S(2)}) collective-permute-start(f32[128,1152]{1,0:T(8,128)S(1)} %collective-permute-done.2.refs_1_), channel_id=1, source_target_pairs={{0,48},{16,0},{32,16},{48,32},{1,49},{17,1},{33,17},{49,33},{2,50}... | collective-permute-start | bytes 1769480 | tf_op jit(solution)/shard_map/ppermute | solution.py:20
  42.3 6.6 %collective-permute-done.6.refs_3_ = f32[128,1152]{1,0:T(8,128)S(1)} collective-permute-done((f32[128,1152]{1,0:T(8,128)S(1)}, f32[128,1152]{1,0:T(8,128)S(1)}, u32[]{:S(2)}, u32[]{:S(2)}) %collective-permute-start.6) | collective-permute-done | bytes 589856 | tf_op jit(solution)/shard_map/ppermute | solution.py:20
  48.9 3.4 %collective-permute-done.4.refs_4_ = f32[128,1152]{1,0:T(8,128)S(1)} collective-permute-done((f32[128,1152]{1,0:T(8,128)S(1)}, f32[128,1152]{1,0:T(8,128)S(1)}, u32[]{:S(2)}, u32[]{:S(2)}) %collective-permute-start.4) | collective-permute-done | bytes 589856 | tf_op jit(solution)/shard_map/ppermute | solution.py:20
  53.4 3.0 %collective-permute-start.10 = (f32[128,1152]{1,0:T(8,128)S(1)}, f32[128,1152]{1,0:T(8,128)S(1)}, u32[]{:S(2)}, u32[]{:S(2)}) collective-permute-start(f32[128,1152]{1,0:T(8,128)S(1)} %collective-permute-done.6.refs_3_), channel_id=1, source_target_pairs={{0,48},{16,0},{32,16},{48,32},{1,49},{17,1},{33,17},{49,33},{2,50}... | collective-permute-start | bytes 1769480 | tf_op jit(solution)/shard_map/ppermute | solution.py:20
  59.9 6.9 %collective-permute-done.10.refs_5_ = f32[128,1152]{1,0:T(8,128)S(1)} collective-permute-done((f32[128,1152]{1,0:T(8,128)S(1)}, f32[128,1152]{1,0:T(8,128)S(1)}, u32[]{:S(2)}, u32[]{:S(2)}) %collective-permute-start.10) | collective-permute-done | bytes 589856 | tf_op jit(solution)/shard_map/ppermute | solution.py:20
  66.9 3.4 %collective-permute-done.8.refs_6_ = f32[128,1152]{1,0:T(8,128)S(1)} collective-permute-done((f32[128,1152]{1,0:T(8,128)S(1)}, f32[128,1152]{1,0:T(8,128)S(1)}, u32[]{:S(2)}, u32[]{:S(2)}) %collective-permute-start.8) | collective-permute-done | bytes 589856 | tf_op jit(solution)/shard_map/ppermute | solution.py:20
  70.4 2.9 %collective-permute-start.12 = (f32[128,1152]{1,0:T(8,128)S(1)}, f32[128,1152]{1,0:T(8,128)S(1)}, u32[]{:S(2)}, u32[]{:S(2)}) collective-permute-start(f32[128,1152]{1,0:T(8,128)S(1)} %collective-permute-done.10.refs_5_), channel_id=1, source_target_pairs={{0,48},{16,0},{32,16},{48,32},{1,49},{17,1},{33,17},{49,33},{2,50}... | collective-permute-start | bytes 1769480 | tf_op jit(solution)/shard_map/ppermute | solution.py:20
  73.3 3.1 %collective-permute-start.13 = (f32[128,1152]{1,0:T(8,128)S(1)}, f32[128,1152]{1,0:T(8,128)S(1)}, u32[]{:S(2)}, u32[]{:S(2)}) collective-permute-start(f32[128,1152]{1,0:T(8,128)S(1)} %collective-permute-done.11), channel_id=1, source_target_pairs={{0,6},{2,0},{4,2},{6,4},{1,7},{3,1},{5,3},{7,5},{8,14},{10,8},{12,... | collective-permute-start | bytes 1769480 | tf_op jit(solution)/shard_map/ppermute | solution.py:20
  78.0 4.3 %collective-permute-done.12.refs_7_ = f32[128,1152]{1,0:T(8,128)S(1)} collective-permute-done((f32[128,1152]{1,0:T(8,128)S(1)}, f32[128,1152]{1,0:T(8,128)S(1)}, u32[]{:S(2)}, u32[]{:S(2)}) %collective-permute-start.12) | collective-permute-done | bytes 589856 | tf_op jit(solution)/shard_map/ppermute | solution.py:20
  94.3 61.6 %shard_map.69 = (f32[128,1152]{1,0:T(8,128)}, f32[128,1152]{1,0:T(8,128)}, f32[128,1152]{1,0:T(8,128)}, f32[128,1152]{1,0:T(8,128)}, f32[128,1152]{1,0:T(8,128)}...) custom-call(s32[16]{0:T(128)} %stack.67.bases, ...), custom_call_target="tpu_custom_call" | custom-call | flops 43486543872 | bytes 28311552 | tf_op jit(solution)/shard_map/pallas_call | solution.py:147
  156.3 2.8 %collective-permute-done.20 = f32[256,1152]{1,0:T(8,128)S(1)} collective-permute-done((f32[256,1152]{1,0:T(8,128)}, f32[256,1152]{1,0:T(8,128)S(1)}, u32[]{:S(2)}, u32[]{:S(2)}) %collective-permute-start.20) | collective-permute-done | bytes 1179680 | tf_op jit(solution)/shard_map/ppermute | solution.py:20
  163.5 9.6 %collective-permute-done.18 = f32[128,1152]{1,0:T(8,128)S(1)} collective-permute-done((f32[128,1152]{1,0:T(8,128)}, f32[128,1152]{1,0:T(8,128)S(1)}, u32[]{:S(2)}, u32[]{:S(2)}) %collective-permute-start.18) | collective-permute-done | bytes 589856 | tf_op jit(solution)/shard_map/ppermute | solution.py:20
  173.2 3.7 %collective-permute-start.22 = (f32[128,1152]{1,0:T(8,128)S(1)}, f32[128,1152]{1,0:T(8,128)S(1)}, u32[]{:S(2)}, u32[]{:S(2)}) collective-permute-start(f32[128,1152]{1,0:T(8,128)S(1)} %get-tuple-element.81), channel_id=1, source_target_pairs={{0,6},{2,0},{4,2},{6,4},{1,7},{3,1},{5,3},{7,5},{8,14},{10,8},{12,... | collective-permute-start | bytes 1769480 | tf_op jit(solution)/shard_map/ppermute | solution.py:20
  179.1 9.9 %collective-permute-done.22 = f32[128,1152]{1,0:T(8,128)S(1)} collective-permute-done((f32[128,1152]{1,0:T(8,128)S(1)}, f32[128,1152]{1,0:T(8,128)S(1)}, u32[]{:S(2)}, u32[]{:S(2)}) %collective-permute-start.22) | collective-permute-done | bytes 589856 | tf_op jit(solution)/shard_map/ppermute | solution.py:20
  191.2 3.8 %collective-permute-start.34 = (f32[128,1152]{1,0:T(8,128)S(1)}, f32[128,1152]{1,0:T(8,128)S(1)}, u32[]{:S(2)}, u32[]{:S(2)}) collective-permute-start(f32[128,1152]{1,0:T(8,128)S(1)} %get-tuple-element.115), channel_id=1, source_target_pairs={{0,6},{2,0},{4,2},{6,4},{1,7},{3,1},{5,3},{7,5},{8,14},{10,8},{12,... | collective-permute-start | bytes 1769480 | tf_op jit(solution)/shard_map/ppermute | solution.py:20
  197.2 5.6 %collective-permute-done.26 = f32[128,1152]{1,0:T(8,128)S(1)} collective-permute-done((f32[128,1152]{1,0:T(8,128)S(1)}, f32[128,1152]{1,0:T(8,128)S(1)}, u32[]{:S(2)}, u32[]{:S(2)}) %collective-permute-start.26) | collective-permute-done | bytes 589856 | tf_op jit(solution)/shard_map/ppermute | solution.py:20
  205.6 2.4 %collective-permute-done.31 = f32[128,1152]{1,0:T(8,128)S(1)} collective-permute-done((f32[128,1152]{1,0:T(8,128)S(1)}, f32[128,1152]{1,0:T(8,128)S(1)}, u32[]{:S(2)}, u32[]{:S(2)}) %collective-permute-start.31) | collective-permute-done | bytes 589856 | tf_op jit(solution)/shard_map/ppermute | solution.py:20
  215.4 4.3 %collective-permute-done.28 = f32[128,1152]{1,0:T(8,128)} collective-permute-done((f32[128,1152]{1,0:T(8,128)}, f32[128,1152]{1,0:T(8,128)}, u32[]{:S(2)}, u32[]{:S(2)}) %collective-permute-start.28) | collective-permute-done | bytes 589856 | tf_op jit(solution)/shard_map/ppermute | solution.py:20
  219.6 3.8 %collective-permute-done.33 = f32[128,1152]{1,0:T(8,128)} collective-permute-done((f32[128,1152]{1,0:T(8,128)}, f32[128,1152]{1,0:T(8,128)}, u32[]{:S(2)}, u32[]{:S(2)}) %collective-permute-start.33) | collective-permute-done | bytes 589856 | tf_op jit(solution)/shard_map/ppermute | solution.py:20
  225.8 3.4 %collective-permute-done.35 = f32[128,1152]{1,0:T(8,128)} collective-permute-done((f32[128,1152]{1,0:T(8,128)}, f32[128,1152]{1,0:T(8,128)}, u32[]{:S(2)}, u32[]{:S(2)}) %collective-permute-start.35) | collective-permute-done | bytes 589856 | tf_op jit(solution)/shard_map/ppermute | solution.py:20
  (135 shorter events, 57.0 us)
Async XLA Ops:
  4.0 16.4 %collective-permute-start.2 = (f32[128,1152]{1,0:T(8,128)}, f32[128,1152]{1,0:T(8,128)S(1)}, u32[]{:S(2)}, u32[]{:S(2)}) collective-permute-start(f32[128,1152]{1,0:T(8,128)} %get-tuple-element.55.refs_0_), channel_id=1, source_target_pairs={{0,64},{64,0},{1,65},{65,1},{2,66},{66,2},{3,67},{67,3},{4,68},{68... | collective-permute-start | bytes 1769480 | tf_op jit(solution)/shard_map/ppermute | solution.py:20
  5.6 16.2 %collective-permute-start = (f32[128,1152]{1,0:T(8,128)}, f32[128,1152]{1,0:T(8,128)S(1)}, u32[]{:S(2)}, u32[]{:S(2)}) collective-permute-start(f32[128,1152]{1,0:T(8,128)} %get-tuple-element.55.refs_0_), channel_id=1, source_target_pairs={{0,16},{16,32},{32,48},{48,0},{1,17},{17,33},{33,49},{49,1},{2,18}... | collective-permute-start | bytes 1769480 | tf_op jit(solution)/shard_map/ppermute | solution.py:20
  7.1 27.3 %collective-permute-start.3 = (f32[128,1152]{1,0:T(8,128)}, f32[128,1152]{1,0:T(8,128)S(1)}, u32[]{:S(2)}, u32[]{:S(2)}) collective-permute-start(f32[128,1152]{1,0:T(8,128)} %get-tuple-element.56), channel_id=1, source_target_pairs={{0,8},{8,0},{1,9},{9,1},{2,10},{10,2},{3,11},{11,3},{4,12},{12,4},... | collective-permute-start | bytes 1769480 | tf_op jit(solution)/shard_map/ppermute | solution.py:20
  10.0 24.4 %collective-permute-start.1 = (f32[128,1152]{1,0:T(8,128)}, f32[128,1152]{1,0:T(8,128)S(1)}, u32[]{:S(2)}, u32[]{:S(2)}) collective-permute-start(f32[128,1152]{1,0:T(8,128)} %get-tuple-element.56), channel_id=1, source_target_pairs={{0,2},{2,4},{4,6},{6,0},{1,3},{3,5},{5,7},{7,1},{8,10},{10,12},{12... | collective-permute-start | bytes 1769480 | tf_op jit(solution)/shard_map/ppermute | solution.py:20
  37.2 15.1 %collective-permute-start.4 = (f32[128,1152]{1,0:T(8,128)S(1)}, f32[128,1152]{1,0:T(8,128)S(1)}, u32[]{:S(2)}, u32[]{:S(2)}) collective-permute-start(f32[128,1152]{1,0:T(8,128)S(1)} %collective-permute-done.refs_2_), channel_id=1, source_target_pairs={{0,16},{16,32},{32,48},{48,0},{1,17},{17,33},{33,49},{49,1},{2,18}... | collective-permute-start | bytes 1769480 | tf_op jit(solution)/shard_map/ppermute | solution.py:20
  37.2 16.2 %collective-permute-start.5 = (f32[128,1152]{1,0:T(8,128)S(1)}, f32[128,1152]{1,0:T(8,128)S(1)}, u32[]{:S(2)}, u32[]{:S(2)}) collective-permute-start(f32[128,1152]{1,0:T(8,128)S(1)} %collective-permute-done.1), channel_id=1, source_target_pairs={{0,2},{2,4},{4,6},{6,0},{1,3},{3,5},{5,7},{7,1},{8,10},{10,12},{12... | collective-permute-start | bytes 1769480 | tf_op jit(solution)/shard_map/ppermute | solution.py:20
  59.7 34.5 %collective-permute-start.14 = (f32[256,1152]{1,0:T(8,128)S(1)}, f32[256,1152]{1,0:T(8,128)}, u32[]{:S(2)}, u32[]{:S(2)}) collective-permute-start(f32[256,1152]{1,0:T(8,128)S(1)} %constant_dynamic-update-slice_fusion.1.refs_8_), channel_id=1, source_target_pairs={{0,1},{1,0},{2,3},{3,2},{4,5},{5,4},{6,7},{7,6},{8,9},{9,8},{10,11... | collective-permute-start | bytes 3538952 | tf_op jit(solution)/shard_map/ppermute | solution.py:20
  76.4 17.9 %collective-permute-start.15 = (f32[256,1152]{1,0:T(8,128)S(1)}, f32[256,1152]{1,0:T(8,128)}, u32[]{:S(2)}, u32[]{:S(2)}) collective-permute-start(f32[256,1152]{1,0:T(8,128)S(1)} %constant_dynamic-update-slice_fusion.3.refs_10_), channel_id=1, source_target_pairs={{0,1},{1,0},{2,3},{3,2},{4,5},{5,4},{6,7},{7,6},{8,9},{9,8},{10,11... | collective-permute-start | bytes 3538952 | tf_op jit(solution)/shard_map/ppermute | solution.py:20
  76.6 17.7 %collective-permute-start.16 = (f32[256,1152]{1,0:T(8,128)S(1)}, f32[256,1152]{1,0:T(8,128)}, u32[]{:S(2)}, u32[]{:S(2)}) collective-permute-start(f32[256,1152]{1,0:T(8,128)S(1)} %constant_dynamic-update-slice_fusion.5.refs_12_), channel_id=1, source_target_pairs={{0,1},{1,0},{2,3},{3,2},{4,5},{5,4},{6,7},{7,6},{8,9},{9,8},{10,11... | collective-permute-start | bytes 3538952 | tf_op jit(solution)/shard_map/ppermute | solution.py:20
  156.3 16.9 %collective-permute-start.18 = (f32[128,1152]{1,0:T(8,128)}, f32[128,1152]{1,0:T(8,128)S(1)}, u32[]{:S(2)}, u32[]{:S(2)}) collective-permute-start(f32[128,1152]{1,0:T(8,128)} %get-tuple-element.73), channel_id=1, source_target_pairs={{0,16},{16,32},{32,48},{48,0},{1,17},{17,33},{33,49},{49,1},{2,18}... | collective-permute-start | bytes 1769480 | tf_op jit(solution)/shard_map/ppermute | solution.py:20
  160.7 28.5 %collective-permute-start.24 = (f32[256,1152]{1,0:T(8,128)S(1)}, f32[256,1152]{1,0:T(8,128)S(1)}, u32[]{:S(2)}, u32[]{:S(2)}) collective-permute-start(f32[256,1152]{1,0:T(8,128)S(1)} %copy-done.15), channel_id=1, source_target_pairs={{0,1},{1,0},{2,3},{3,2},{4,5},{5,4},{6,7},{7,6},{8,9},{9,8},{10,11... | collective-permute-start | bytes 3538952 | tf_op jit(solution)/shard_map/ppermute | solution.py:20
  161.1 29.2 %collective-permute-start.30 = (f32[256,1152]{1,0:T(8,128)S(1)}, f32[256,1152]{1,0:T(8,128)S(1)}, u32[]{:S(2)}, u32[]{:S(2)}) collective-permute-start(f32[256,1152]{1,0:T(8,128)S(1)} %copy-done.14), channel_id=1, source_target_pairs={{0,1},{1,0},{2,3},{3,2},{4,5},{5,4},{6,7},{7,6},{8,9},{9,8},{10,11... | collective-permute-start | bytes 3538952 | tf_op jit(solution)/shard_map/ppermute | solution.py:20
  161.3 15.5 %collective-permute-start.19 = (f32[128,1152]{1,0:T(8,128)S(1)}, f32[128,1152]{1,0:T(8,128)S(1)}, u32[]{:S(2)}, u32[]{:S(2)}) collective-permute-start(f32[128,1152]{1,0:T(8,128)S(1)} %copy-done.24), channel_id=1, source_target_pairs={{0,48},{16,0},{32,16},{48,32},{1,49},{17,1},{33,17},{49,33},{2,50}... | collective-permute-start | bytes 1769480 | tf_op jit(solution)/shard_map/ppermute | solution.py:20
  162.7 16.4 %collective-permute-start.21 = (f32[128,1152]{1,0:T(8,128)S(1)}, f32[128,1152]{1,0:T(8,128)S(1)}, u32[]{:S(2)}, u32[]{:S(2)}) collective-permute-start(f32[128,1152]{1,0:T(8,128)S(1)} %get-tuple-element.80), channel_id=1, source_target_pairs={{0,2},{2,4},{4,6},{6,0},{1,3},{3,5},{5,7},{7,1},{8,10},{10,12},{12... | collective-permute-start | bytes 1769480 | tf_op jit(solution)/shard_map/ppermute | solution.py:20
  173.2 15.8 %collective-permute-start.22 = (f32[128,1152]{1,0:T(8,128)S(1)}, f32[128,1152]{1,0:T(8,128)S(1)}, u32[]{:S(2)}, u32[]{:S(2)}) collective-permute-start(f32[128,1152]{1,0:T(8,128)S(1)} %get-tuple-element.81), channel_id=1, source_target_pairs={{0,6},{2,0},{4,2},{6,4},{1,7},{3,1},{5,3},{7,5},{8,14},{10,8},{12,... | collective-permute-start | bytes 1769480 | tf_op jit(solution)/shard_map/ppermute | solution.py:20
  176.9 18.2 %collective-permute-start.25 = (f32[128,1152]{1,0:T(8,128)S(1)}, f32[128,1152]{1,0:T(8,128)S(1)}, u32[]{:S(2)}, u32[]{:S(2)}) collective-permute-start(f32[128,1152]{1,0:T(8,128)S(1)} %copy-done.23), channel_id=1, source_target_pairs={{0,16},{16,32},{32,48},{48,0},{1,17},{17,33},{33,49},{49,1},{2,18}... | collective-permute-start | bytes 1769480 | tf_op jit(solution)/shard_map/ppermute | solution.py:20
  190.3 17.7 %collective-permute-start.31 = (f32[128,1152]{1,0:T(8,128)S(1)}, f32[128,1152]{1,0:T(8,128)S(1)}, u32[]{:S(2)}, u32[]{:S(2)}) collective-permute-start(f32[128,1152]{1,0:T(8,128)S(1)} %get-tuple-element.112), channel_id=1, source_target_pairs={{0,2},{2,4},{4,6},{6,0},{1,3},{3,5},{5,7},{7,1},{8,10},{10,12},{12... | collective-permute-start | bytes 1769480 | tf_op jit(solution)/shard_map/ppermute | solution.py:20
  191.2 18.6 %collective-permute-start.34 = (f32[128,1152]{1,0:T(8,128)S(1)}, f32[128,1152]{1,0:T(8,128)S(1)}, u32[]{:S(2)}, u32[]{:S(2)}) collective-permute-start(f32[128,1152]{1,0:T(8,128)S(1)} %get-tuple-element.115), channel_id=1, source_target_pairs={{0,6},{2,0},{4,2},{6,4},{1,7},{3,1},{5,3},{7,5},{8,14},{10,8},{12,... | collective-permute-start | bytes 1769480 | tf_op jit(solution)/shard_map/ppermute | solution.py:20
  195.0 16.9 %collective-permute-start.23 = (f32[128,1152]{1,0:T(8,128)S(1)}, f32[128,1152]{1,0:T(8,128)S(1)}, u32[]{:S(2)}, u32[]{:S(2)}) collective-permute-start(f32[128,1152]{1,0:T(8,128)S(1)} %add.416), channel_id=1, source_target_pairs={{0,16},{16,32},{32,48},{48,0},{1,17},{17,33},{33,49},{49,1},{2,18}... | collective-permute-start | bytes 1769480 | tf_op jit(solution)/shard_map/ppermute | solution.py:20
  203.8 15.8 %collective-permute-start.28 = (f32[128,1152]{1,0:T(8,128)}, f32[128,1152]{1,0:T(8,128)}, u32[]{:S(2)}, u32[]{:S(2)}) collective-permute-start(f32[128,1152]{1,0:T(8,128)} %add_add_fusion), channel_id=1, source_target_pairs={{0,64},{64,0},{1,65},{65,1},{2,66},{66,2},{3,67},{67,3},{4,68},{68... | collective-permute-start | bytes 1769480 | tf_op jit(solution)/shard_map/ppermute | solution.py:20
  203.9 15.7 %collective-permute-start.27 = (f32[128,1152]{1,0:T(8,128)}, f32[128,1152]{1,0:T(8,128)}, u32[]{:S(2)}, u32[]{:S(2)}) collective-permute-start(f32[128,1152]{1,0:T(8,128)} %get-tuple-element.89), channel_id=1, source_target_pairs={{0,48},{16,0},{32,16},{48,32},{1,49},{17,1},{33,17},{49,33},{2,50}... | collective-permute-start | bytes 1769480 | tf_op jit(solution)/shard_map/ppermute | solution.py:20
  208.0 15.5 %collective-permute-start.33 = (f32[128,1152]{1,0:T(8,128)}, f32[128,1152]{1,0:T(8,128)}, u32[]{:S(2)}, u32[]{:S(2)}) collective-permute-start(f32[128,1152]{1,0:T(8,128)} %get-tuple-element.104), channel_id=1, source_target_pairs={{0,6},{2,0},{4,2},{6,4},{1,7},{3,1},{5,3},{7,5},{8,14},{10,8},{12,... | collective-permute-start | bytes 1769480 | tf_op jit(solution)/shard_map/ppermute | solution.py:20
  209.7 16.0 %collective-permute-start.32 = (f32[128,1152]{1,0:T(8,128)S(1)}, f32[128,1152]{1,0:T(8,128)}, u32[]{:S(2)}, u32[]{:S(2)}) collective-permute-start(f32[128,1152]{1,0:T(8,128)S(1)} %get-tuple-element.103), channel_id=1, source_target_pairs={{0,2},{2,4},{4,6},{6,0},{1,3},{3,5},{5,7},{7,1},{8,10},{10,12},{12... | collective-permute-start | bytes 1769480 | tf_op jit(solution)/shard_map/ppermute | solution.py:20
  212.8 16.4 %collective-permute-start.35 = (f32[128,1152]{1,0:T(8,128)}, f32[128,1152]{1,0:T(8,128)}, u32[]{:S(2)}, u32[]{:S(2)}) collective-permute-start(f32[128,1152]{1,0:T(8,128)} %fusion), channel_id=1, source_target_pairs={{0,8},{8,0},{1,9},{9,1},{2,10},{10,2},{3,11},{11,3},{4,12},{12,4},... | collective-permute-start | bytes 1769480 | tf_op jit(solution)/shard_map/ppermute | solution.py:20
  (37 other events, 468.7 us)

commit v3 on v2

--- a/solution.py
+++ b/solution.py
@@ -12,7 +12,7 @@
 F32 = jnp.float32
 BF16 = jnp.bfloat16
 AXES = ("yl", "x", "yh", "z", "c")
-PLACES = ((0, 0), (0, 1), (-1, 0), (1, 1), (2, 0), (2, 1), (1, 0), (-1, 1))
+PLACES = ((0, 0), (0, 1), (-1, 0), (1, 0), (2, 0), (2, 1), (1, 1), (-1, 1))
 
 
 def shift_by(value, axis, steps):
@@ -51,11 +51,12 @@
     )(warmth.reshape(1, 1), photo, text)
 
 
-def pairs_kernel(bases, shift, match, *refs, shares, parts, n, ti, tj):
+def pairs_kernel(bases, shift, match, *refs, shares, parts, n, ti, tj, more):
     imgs, refs = refs[:shares], refs[shares:]
+    gi_in, refs = refs[: shares * more], refs[shares * more :]
     count = sum(len(p) for p in parts)
     txts, gi_out, gt_out = refs[:count], refs[count : count + shares], refs[count + shares : 2 * count + shares]
-    gi, gt, raw, ah, al, bh, bl, img_in, img_out, txt_in, txt_out = refs[2 * count + shares :]
+    gi, gt, raw, ah, al, bh, bl, img_in, img_out, sum_in, txt_in, txt_out = refs[2 * count + shares :]
     j = pl.program_id(0)
     last = len(parts) - 1
 
@@ -77,14 +78,21 @@
 
     @pl.when(j == 0)
     def _():
-        copies = [pltpu.make_async_copy(imgs[k], gi.at[pl.ds(k * n, n)], img_in.at[k]) for k in range(shares)]
-        for c in copies + text_in(0):
+        per = tj // n
+        copies = [
+            pltpu.make_async_copy(imgs[k], gt.at[k // per, pl.ds(k % per * n, n)], img_in.at[k]) for k in range(shares)
+        ]
+        sums = [pltpu.make_async_copy(gi_in[k], gi.at[pl.ds(k * n, n)], sum_in.at[k]) for k in range(shares * more)]
+        for c in copies + text_in(0) + sums:
             c.start()
         for k, c in enumerate(copies):
             c.wait()
             rows = pl.ds(k * n, n)
-            ah[rows, :], al[rows, :] = halves(gi[rows, :])
-        gi[...] = jnp.zeros_like(gi)
+            ah[rows, :], al[rows, :] = halves(gt[k // per, pl.ds(k % per * n, n), :])
+        for c in sums:
+            c.wait()
+        if not more:
+            gi[...] = jnp.zeros_like(gi)
 
     for k in range(last + 1):
 
@@ -138,80 +146,74 @@
             c.wait()
 
 
-def pair_gradients(shift, imgs, match, txts, parts, bases, ti=512):
+def pair_gradients(shift, imgs, match, txts, parts, bases, sums=(), ti=512):
     n, d = imgs[0].shape
     rows, tj = len(imgs) * n, sum(q[1] for q in parts[0])
     cols = len(parts) * tj
     sm, vm, far = (pl.BlockSpec(memory_space=m) for m in (pltpu.SMEM, pltpu.VMEM, pl.ANY))
     out = [jax.ShapeDtypeStruct(x.shape, F32) for x in (*imgs, *txts)]
     out = pl.pallas_call(
-        functools.partial(pairs_kernel, shares=len(imgs), parts=parts, n=n, ti=ti, tj=tj),
+        functools.partial(pairs_kernel, shares=len(imgs), parts=parts, n=n, ti=ti, tj=tj, more=int(len(sums) > 0)),
         grid=(len(parts),),
-        in_specs=[sm, sm, vm] + [far] * len(out),
+        in_specs=[sm, sm, vm] + [far] * (len(out) + len(sums)),
         out_specs=[far] * len(out),
         scratch_shapes=[pltpu.VMEM((rows, d), F32)]
         + [pltpu.VMEM((2, tj, d), F32)] * 2
         + [pltpu.VMEM((rows, d), BF16)] * 2
         + [pltpu.VMEM((tj, d), BF16)] * 2
-        + [pltpu.SemaphoreType.DMA((len(imgs),))] * 2
+        + [pltpu.SemaphoreType.DMA((len(imgs),))] * 3
         + [pltpu.SemaphoreType.DMA((2, 2))] * 2,
         out_shape=out,
         compiler_params=pltpu.CompilerParams(vmem_limit_bytes=58 * 2**20),
         cost_estimate=pl.CostEstimate(
             flops=18 * rows * cols * d, bytes_accessed=8 * (rows + cols) * d, transcendentals=2 * rows * cols
         ),
-    )(bases, shift, match, *imgs, *txts)
+    )(bases, shift, match, *imgs, *sums, *txts)
     return out[: len(imgs)], out[len(imgs) :]
 
 
-def gather_shares(photo, text):
+def gather_shares(photo, text, index):
     hold = lax.optimization_barrier
-    ups, downs = [(photo, text)], []
-    up, down = hold(
-        (
-            (shift_by(photo, "x", 1), shift_by(text, "z", 1)),
-            (shift_by(photo, "yl", 1), shift_by(text, "yh", 1)),
-        )
-    )
-    for hop in range(3):
-        ups.append(up)
-        downs.append(down)
-        nxt = tuple(shift_by(v, a, -1) for v, a in zip(down, ("x", "z")))
-        if hop < 2:
-            up, down = hold((tuple(shift_by(v, a, 1) for v, a in zip(up, ("x", "z"))), nxt))
-        else:
-            downs.append(hold(nxt))
-    return ([pair[k] for both in zip(ups, downs) for pair in both] for k in (0, 1))
-
-
-def reduce_shares(photo, text_mine, text_other):
+    i_back, i_front = shift_by(photo, "x", 1), shift_by(photo, "x", -1)
+    t_back, t_front = shift_by(text, "z", 1), shift_by(text, "z", -1)
+    i_twin = shift_by(photo, "yl", 1)
+    i_back, i_front, t_back, t_front, i_twin, text, index = hold((i_back, i_front, t_back, t_front, i_twin, text, index))
+    t_twin = shift_by(text, "yh", 1)
+    i_far, t_far = shift_by(i_back, "x", 1), shift_by(t_back, "z", 1)
+    i_twin_front = shift_by(i_twin, "x", -1)
+    t_twin, i_far, t_far, i_twin_front, i_twin = hold((t_twin, i_far, t_far, i_twin_front, i_twin))
+    t_twin_front, t_twin_back = shift_by(t_twin, "z", -1), shift_by(t_twin, "z", 1)
+    i_twin_far, i_twin_back = shift_by(i_twin_front, "x", -1), shift_by(i_twin, "x", 1)
+    t_twin_front, t_twin_back, i_twin_far, i_twin_back = hold((t_twin_front, t_twin_back, i_twin_far, i_twin_back))
+    t_twin_far = shift_by(t_twin_front, "z", -1)
+    imgs = [photo, i_twin, i_back, i_front, i_far, i_twin_far, i_twin_front, i_twin_back]
+    txts = [text, t_twin, t_back, t_front, t_far, t_twin_far, t_twin_front, t_twin_back]
+    return imgs, txts, index
+
+
+def split_rows(x, n):
+    return [x[k : k + n] for k in range(0, x.shape[0], n)]
+
+
+def reduce_shares(photo, text_near, text_far):
     hold = lax.optimization_barrier
-    i_own, i_twin, i_back, i_twin_front, i_far, i_twin_far, i_front, i_twin_back = photo
+    i_own, i_twin, i_back, i_front, i_far, i_twin_far, i_twin_front, i_twin_back = photo
     n = i_own.shape[0]
-
-    def join(k, other):
-        both = text_mine[k] + shift_by(other, "c", 1)
-        return both[:n], both[n:]
-
     i_up, i_down = shift_by(i_far, "x", 1), shift_by(i_twin_far, "x", -1)
-    t_far, t_twin_far = join(2, text_other[2])
-    rest = (text_other[0], text_other[1], text_other[3])
-    rest, t_far, t_twin_far = hold((rest, t_far, t_twin_far))
+    near, far = shift_by(text_near[1], "c", 1), text_far[1]
+    near, far = hold((near, far))
+    t_far, t_twin_far, t_twin_front, t_twin_back = split_rows(text_far[0] + shift_by(far, "c", 1), n)
     t_up, t_down = shift_by(t_far, "z", 1), shift_by(t_twin_far, "z", -1)
-    i_up, i_down, t_up, t_down = hold((i_up, i_down, t_up, t_down))
-    t_back, t_twin_front = join(1, rest[1])
-    t_front, t_twin_back = join(3, rest[2])
+    t_own, t_twin, t_back, t_front = split_rows(text_near[0] + near, n)
+    i_up, i_down, t_up, t_down, t_back = hold((i_up, i_down, t_up, t_down, t_back))
     i_p, i_q = shift_by(i_twin_front, "x", 1), shift_by(i_twin_back + i_down, "x", -1)
-    near, t_up, t_down = hold((rest[0], t_up, t_down))
-    t_own, t_twin = join(0, near)
     t_p, t_q = shift_by(t_twin_front, "z", 1), shift_by(t_twin_back + t_down, "z", -1)
-    i_back, t_back, i_p, i_q = hold((i_back, t_back, i_p, i_q))
+    t_s = shift_by(t_back, "z", -1)
+    i_back, i_p, i_q, t_p, t_q = hold((i_back, i_p, i_q, t_p, t_q))
     i_y = shift_by(i_twin + i_p + i_q, "yl", 1)
+    t_y = shift_by(t_twin + t_p + t_q, "yh", 1)
     i_r, i_s = shift_by(i_front + i_up, "x", 1), shift_by(i_back, "x", -1)
-    t_s = shift_by(t_back, "z", -1)
-    t_front, t_p = hold((t_front + t_up, t_p))
-    t_y = shift_by(t_twin + t_p + t_q, "yh", 1)
-    t_r = shift_by(t_front, "z", 1)
+    t_r = shift_by(t_front + t_up, "z", 1)
     return i_own + i_r + i_s + i_y, t_own + t_r + t_s + t_y
 
 
@@ -227,22 +229,24 @@
     ncol = lax.axis_size("yh") * nz * 2
     photo_scaled, photo_unit, photo_len, text_unit, text_len = normalize(warmth, photo, text)
 
-    imgs, txts = gather_shares(photo_scaled, text_unit)
-    txts = [jnp.concatenate(txts[k : k + 2]) for k in range(0, 8, 2)]
-    txts = [t for own in txts for t in (own, shift_by(own, "c", 1))]
-    parts = [((2 * k, 2 * n), (2 * k + 1, 2 * n)) for k in range(4)]
-
     col = (yh * nz + z) * 2 + c
     row = yl * nx + x
     places = [(yl ^ dy) * nx + (x + dx) % nx for dx, dy in PLACES]
     match = jnp.concatenate([lax.dynamic_slice(matching_index, ((r * ncol + col) * n,), (n,)) for r in places])
-    match = match[:, None]
     mine, other = ([((yh ^ dy) * nz + (z + dz) % nz) * 2 + (c ^ k) for dz, dy in PLACES] for k in (0, 1))
-    cols = [q for k in range(0, 8, 2) for q in mine[k : k + 2] + other[k : k + 2]]
+    cols = mine[:4] + other[:4] + mine[4:] + other[4:]
     bases = jnp.stack([(row * ncol + q) * n for q in cols]).astype(jnp.int32)
 
-    gi, gt = pair_gradients(shift, imgs, match, txts, parts, bases)
-    photo_grad, text_grad = reduce_shares(gi, gt[0::2], gt[1::2])
+    imgs, txts, (match, bases) = gather_shares(photo_scaled, text_unit, (match[:, None], bases))
+    near = jnp.concatenate(txts[:4])
+    near = (near, shift_by(near, "c", 1))
+    parts = [((k, 4 * n),) for k in (0, 1)]
+    gi, gt_near = pair_gradients(shift, imgs, match, near, parts, bases[:8])
+    gi, last = lax.optimization_barrier((gi, txts[5]))
+    far = jnp.concatenate([txts[4], last, *txts[6:]])
+    far = (far, shift_by(far, "c", 1))
+    gi, gt_far = pair_gradients(shift, imgs, match, far, parts, bases[8:], sums=gi)
+    photo_grad, text_grad = reduce_shares(gi, gt_near, gt_far)
     photo_grad = photo_grad * jnp.exp(warmth)
     return restore(photo_grad, photo_unit, photo_len), restore(text_grad, text_unit, text_len)
 

time: 234 us -> 223 us (0.953)
  waiting for transfers between devices: 98.1 us -> 82.2 us
  Pallas kernels: 64.3 us -> 73.1 us
  starting transfers between devices: 45.1 us -> 36.7 us
  local copies, waits for them, and re-layouts: 13.3 us -> 16.6 us
    ppermute x36 -> x32, waiting for transfers between devices: 98.1 us -> 82.2 us  [shift_by(): lax.ppermute(value, axis, [(i, (i + steps) % count) for i in range(count)])]
    pallas_call x1 -> x2, Pallas kernels: 61.6 us -> 70.4 us  [pair_gradients(): pl.pallas_call(functools.partial(pairs_kernel, shares=len(imgs), parts=pa...]
    ppermute x36 -> x32, starting transfers between devices: 45.1 us -> 36.7 us  [shift_by(): lax.ppermute(value, axis, [(i, (i + steps) % count) for i in range(count)])]
    unnamed x61 -> x45, local copies, waits for them, and re-layouts: 8.89 us -> 12.3 us
  transfers between devices with their start and end apart: 36 -> 32, of which waited for: 22 -> 22; matrix products, arithmetic and copies ran while one was open for 8% -> 8% of each run, Pallas kernels for 0% -> 32%
where the time goes in v3:
time: 223 us; the launch traced here: 222 us
  waiting for transfers between devices  82.2 us (37%)
  Pallas kernels  73.1 us (33%)
  starting transfers between devices  36.7 us (16%)
  local copies, waits for them, and re-layouts  16.6 us (7%)
  other arithmetic  11 us (5%)
    ppermute x32, waiting for transfers between devices, shift_by(): lax.ppermute(value, axis, [(i, (i + steps) % count) for i in range(count)])  82.2 us
    pallas_call x2, Pallas kernels, pair_gradients(): pl.pallas_call(functools.partial(pairs_kernel, shares=len(imgs), parts=pa...  70.4 us
    ppermute x32, starting transfers between devices, shift_by(): lax.ppermute(value, axis, [(i, (i + steps) % count) for i in range(count)])  36.7 us
    unnamed x45, local copies, waits for them, and re-layouts  12.3 us
  transfers between devices with their start and end apart: 32, of which 22 were waited for; matrix products, arithmetic and copies ran while one was open for 8% of the time, Pallas kernels for 32%

profile of v3, /device:TPU:0, one launch (start us, length us, event | category | flops | bytes accessed | tf_op | source)
XLA Modules:
  0.0 221.9 jit_solution(9987294003132461099)
XLA Ops:
  1.3 2.7 %shard_map.68 = (f32[128,1152]{1,0:T(8,128)}, f32[128,1152]{1,0:T(8,128)}, f32[128,1]{1,0:T(8,128)}, f32[128,1152]{1,0:T(8,128)}, f32[128,1]{1,0:T(8,128)}) custom-call(f32[1,1]{1,0:T(1,128)} %bitcast.19.warmth, f32[128,1152]{1,0:T(8,128)} %photo.1, f32[128,1152]{1,0:T(8,128)} %text.1), custom_call_target="tpu_custom_call" | custom-call | tf_op jit(solution)/shard_map/pallas_call | solution.py:46
  5.6 2.8 %collective-permute-start.1 = (f32[128,1152]{1,0:T(8,128)}, f32[128,1152]{1,0:T(8,128)S(1)}, u32[]{:S(2)}, u32[]{:S(2)}) collective-permute-start(f32[128,1152]{1,0:T(8,128)} %get-tuple-element.65.refs_0_), channel_id=1, source_target_pairs={{0,48},{16,0},{32,16},{48,32},{1,49},{17,1},{33,17},{49,33},{2,50}... | collective-permute-start | bytes 1769480 | tf_op jit(solution)/shard_map/ppermute | solution.py:20
  8.4 4.0 %collective-permute-start.3 = (f32[128,1152]{1,0:T(8,128)}, f32[128,1152]{1,0:T(8,128)S(1)}, u32[]{:S(2)}, u32[]{:S(2)}) collective-permute-start(f32[128,1152]{1,0:T(8,128)} %get-tuple-element.69), channel_id=1, source_target_pairs={{0,6},{2,0},{4,2},{6,4},{1,7},{3,1},{5,3},{7,5},{8,14},{10,8},{12,... | collective-permute-start | bytes 1769480 | tf_op jit(solution)/shard_map/ppermute | solution.py:20
  21.0 3.3 %collective-permute-done.refs_2_ = f32[128,1152]{1,0:T(8,128)S(1)} collective-permute-done((f32[128,1152]{1,0:T(8,128)}, f32[128,1152]{1,0:T(8,128)S(1)}, u32[]{:S(2)}, u32[]{:S(2)}) %collective-permute-start) | collective-permute-done | bytes 589856 | tf_op jit(solution)/shard_map/ppermute | solution.py:20
  24.8 3.3 %collective-permute-done.2 = f32[128,1152]{1,0:T(8,128)S(1)} collective-permute-done((f32[128,1152]{1,0:T(8,128)}, f32[128,1152]{1,0:T(8,128)S(1)}, u32[]{:S(2)}, u32[]{:S(2)}) %collective-permute-start.2) | collective-permute-done | bytes 589856 | tf_op jit(solution)/shard_map/ppermute | solution.py:20
  28.1 2.9 %collective-permute-start.5 = (f32[128,1152]{1,0:T(8,128)}, f32[128,1152]{1,0:T(8,128)S(1)}, u32[]{:S(2)}, u32[]{:S(2)}) collective-permute-start(f32[128,1152]{1,0:T(8,128)} %get-tuple-element.69), channel_id=1, source_target_pairs={{0,8},{8,0},{1,9},{9,1},{2,10},{10,2},{3,11},{11,3},{4,12},{12,4},... | collective-permute-start | bytes 1769480 | tf_op jit(solution)/shard_map/ppermute | solution.py:20
  31.0 3.0 %collective-permute-start.8 = (f32[128,1152]{1,0:T(8,128)S(1)}, f32[128,1152]{1,0:T(8,128)}, u32[]{:S(2)}, u32[]{:S(2)}) collective-permute-start(f32[128,1152]{1,0:T(8,128)S(1)} %collective-permute-done.4.refs_1_), channel_id=1, source_target_pairs={{0,48},{16,0},{32,16},{48,32},{1,49},{17,1},{33,17},{49,33},{2,50}... | collective-permute-start | bytes 1769480 | tf_op jit(solution)/shard_map/ppermute | solution.py:20
  35.9 7.2 %collective-permute-done.5 = f32[128,1152]{1,0:T(8,128)S(1)} collective-permute-done((f32[128,1152]{1,0:T(8,128)}, f32[128,1152]{1,0:T(8,128)S(1)}, u32[]{:S(2)}, u32[]{:S(2)}) %collective-permute-start.5) | collective-permute-done | bytes 589856 | tf_op jit(solution)/shard_map/ppermute | solution.py:20
  50.3 3.1 %collective-permute-start.9 = (f32[128,1152]{1,0:T(8,128)S(1)}, f32[128,1152]{1,0:T(8,128)S(1)}, u32[]{:S(2)}, u32[]{:S(2)}) collective-permute-start(f32[128,1152]{1,0:T(8,128)S(1)} %collective-permute-done.5), channel_id=1, source_target_pairs={{0,6},{2,0},{4,2},{6,4},{1,7},{3,1},{5,3},{7,5},{8,14},{10,8},{12,... | collective-permute-start | bytes 1769480 | tf_op jit(solution)/shard_map/ppermute | solution.py:20
  53.5 3.2 %collective-permute-start.11 = (f32[128,1152]{1,0:T(8,128)}, f32[128,1152]{1,0:T(8,128)}, u32[]{:S(2)}, u32[]{:S(2)}) collective-permute-start(f32[128,1152]{1,0:T(8,128)} %collective-permute-done.8.refs_6_), channel_id=1, source_target_pairs={{0,48},{16,0},{32,16},{48,32},{1,49},{17,1},{33,17},{49,33},{2,50}... | collective-permute-start | bytes 1769480 | tf_op jit(solution)/shard_map/ppermute | solution.py:20
  59.9 7.3 %collective-permute-done.12.refs_7_ = f32[128,1152]{1,0:T(8,128)S(1)} collective-permute-done((f32[128,1152]{1,0:T(8,128)S(1)}, f32[128,1152]{1,0:T(8,128)S(1)}, u32[]{:S(2)}, u32[]{:S(2)}) %collective-permute-start.12) | collective-permute-done | bytes 589856 | tf_op jit(solution)/shard_map/ppermute | solution.py:20
  71.2 34.7 %shard_map.69 = (f32[128,1152]{1,0:T(8,128)}, f32[128,1152]{1,0:T(8,128)}, f32[128,1152]{1,0:T(8,128)}, f32[128,1152]{1,0:T(8,128)}, f32[128,1152]{1,0:T(8,128)}...) custom-call(s32[8]{0:T(128)} %get-tuple-element.138.bases, ...), custom_call_target="tpu_custom_call" | custom-call | flops 21743271936 | bytes 18874368 | tf_op jit(solution)/shard_map/pallas_call | solution.py:155
  106.7 4.3 %collective-permute-done.15.refs_17_ = f32[512,1152]{1,0:T(8,128)S(1)} collective-permute-done((f32[512,1152]{1,0:T(8,128)S(1)}, f32[512,1152]{1,0:T(8,128)S(1)}, u32[]{:S(2)}, u32[]{:S(2)}) %collective-permute-start.15) | collective-permute-done | bytes 2359328 | tf_op jit(solution)/shard_map/ppermute | solution.py:20
  112.4 35.7 %shard_map.70 = (f32[128,1152]{1,0:T(8,128)}, f32[128,1152]{1,0:T(8,128)}, f32[128,1152]{1,0:T(8,128)}, f32[128,1152]{1,0:T(8,128)}, f32[128,1152]{1,0:T(8,128)}...) custom-call(s32[8]{0:T(128)} %get-tuple-element.139.bases, ...), custom_call_target="tpu_custom_call" | custom-call | flops 21743271936 | bytes 18874368 | tf_op jit(solution)/shard_map/pallas_call | solution.py:155
  148.3 3.7 %collective-permute-start.17 = (f32[128,1152]{1,0:T(8,128)}, f32[128,1152]{1,0:T(8,128)S(1)}, u32[]{:S(2)}, u32[]{:S(2)}) collective-permute-start(f32[128,1152]{1,0:T(8,128)} %get-tuple-element.104), channel_id=1, source_target_pairs={{0,48},{16,0},{32,16},{48,32},{1,49},{17,1},{33,17},{49,33},{2,50}... | collective-permute-start | bytes 1769480 | tf_op jit(solution)/shard_map/ppermute | solution.py:20
  158.3 8.1 %collective-permute-done.16 = f32[128,1152]{1,0:T(8,128)S(1)} collective-permute-done((f32[128,1152]{1,0:T(8,128)}, f32[128,1152]{1,0:T(8,128)S(1)}, u32[]{:S(2)}, u32[]{:S(2)}) %collective-permute-start.16) | collective-permute-done | bytes 589856 | tf_op jit(solution)/shard_map/ppermute | solution.py:20
  166.4 4.1 %collective-permute-done.21 = f32[128,1152]{1,0:T(8,128)S(1)} collective-permute-done((f32[128,1152]{1,0:T(8,128)S(1)}, f32[128,1152]{1,0:T(8,128)S(1)}, u32[]{:S(2)}, u32[]{:S(2)}) %collective-permute-start.21) | collective-permute-done | bytes 589856 | tf_op jit(solution)/shard_map/ppermute | solution.py:20
  172.6 3.2 %collective-permute-start.24 = (f32[128,1152]{1,0:T(8,128)S(1)}, f32[128,1152]{1,0:T(8,128)S(1)}, u32[]{:S(2)}, u32[]{:S(2)}) collective-permute-start(f32[128,1152]{1,0:T(8,128)S(1)} %add.413), channel_id=1, source_target_pairs={{0,48},{16,0},{32,16},{48,32},{1,49},{17,1},{33,17},{49,33},{2,50}... | collective-permute-start | bytes 1769480 | tf_op jit(solution)/shard_map/ppermute | solution.py:20
  179.4 8.1 %collective-permute-done.24 = f32[128,1152]{1,0:T(8,128)S(1)} collective-permute-done((f32[128,1152]{1,0:T(8,128)S(1)}, f32[128,1152]{1,0:T(8,128)S(1)}, u32[]{:S(2)}, u32[]{:S(2)}) %collective-permute-start.24) | collective-permute-done | bytes 589856 | tf_op jit(solution)/shard_map/ppermute | solution.py:20
  187.6 4.4 %collective-permute-done.26 = f32[128,1152]{1,0:T(8,128)S(1)} collective-permute-done((f32[128,1152]{1,0:T(8,128)S(1)}, f32[128,1152]{1,0:T(8,128)S(1)}, u32[]{:S(2)}, u32[]{:S(2)}) %collective-permute-start.26) | collective-permute-done | bytes 589856 | tf_op jit(solution)/shard_map/ppermute | solution.py:20
  198.6 3.9 %collective-permute-done.30 = f32[128,1152]{1,0:T(8,128)} collective-permute-done((f32[128,1152]{1,0:T(8,128)}, f32[128,1152]{1,0:T(8,128)}, u32[]{:S(2)}, u32[]{:S(2)}) %collective-permute-start.30) | collective-permute-done | bytes 589856 | tf_op jit(solution)/shard_map/ppermute | solution.py:20
  202.5 4.4 %collective-permute-done.29 = f32[128,1152]{1,0:T(8,128)} collective-permute-done((f32[128,1152]{1,0:T(8,128)}, f32[128,1152]{1,0:T(8,128)}, u32[]{:S(2)}, u32[]{:S(2)}) %collective-permute-start.29) | collective-permute-done | bytes 589856 | tf_op jit(solution)/shard_map/ppermute | solution.py:20
  207.0 4.8 %collective-permute-done.31 = f32[128,1152]{1,0:T(8,128)} collective-permute-done((f32[128,1152]{1,0:T(8,128)}, f32[128,1152]{1,0:T(8,128)}, u32[]{:S(2)}, u32[]{:S(2)}) %collective-permute-start.31) | collective-permute-done | bytes 589856 | tf_op jit(solution)/shard_map/ppermute | solution.py:20
  211.8 5.7 %collective-permute-done.28 = f32[128,1152]{1,0:T(8,128)} collective-permute-done((f32[128,1152]{1,0:T(8,128)}, f32[128,1152]{1,0:T(8,128)}, u32[]{:S(2)}, u32[]{:S(2)}) %collective-permute-start.28) | collective-permute-done | bytes 589856 | tf_op jit(solution)/shard_map/ppermute | solution.py:20
  (109 shorter events, 51.7 us)
Async XLA Ops:
  4.0 15.2 %collective-permute-start.4 = (f32[128,1152]{1,0:T(8,128)}, f32[128,1152]{1,0:T(8,128)S(1)}, u32[]{:S(2)}, u32[]{:S(2)}) collective-permute-start(f32[128,1152]{1,0:T(8,128)} %get-tuple-element.65.refs_0_), channel_id=1, source_target_pairs={{0,64},{64,0},{1,65},{65,1},{2,66},{66,2},{3,67},{67,3},{4,68},{68... | collective-permute-start | bytes 1769480 | tf_op jit(solution)/shard_map/ppermute | solution.py:20
  5.6 15.4 %collective-permute-start.1 = (f32[128,1152]{1,0:T(8,128)}, f32[128,1152]{1,0:T(8,128)S(1)}, u32[]{:S(2)}, u32[]{:S(2)}) collective-permute-start(f32[128,1152]{1,0:T(8,128)} %get-tuple-element.65.refs_0_), channel_id=1, source_target_pairs={{0,48},{16,0},{32,16},{48,32},{1,49},{17,1},{33,17},{49,33},{2,50}... | collective-permute-start | bytes 1769480 | tf_op jit(solution)/shard_map/ppermute | solution.py:20
  8.4 15.9 %collective-permute-start = (f32[128,1152]{1,0:T(8,128)}, f32[128,1152]{1,0:T(8,128)S(1)}, u32[]{:S(2)}, u32[]{:S(2)}) collective-permute-start(f32[128,1152]{1,0:T(8,128)} %get-tuple-element.65.refs_0_), channel_id=1, source_target_pairs={{0,16},{16,32},{32,48},{48,0},{1,17},{17,33},{33,49},{49,1},{2,18}... | collective-permute-start | bytes 1769480 | tf_op jit(solution)/shard_map/ppermute | solution.py:20
  8.4 16.4 %collective-permute-start.3 = (f32[128,1152]{1,0:T(8,128)}, f32[128,1152]{1,0:T(8,128)S(1)}, u32[]{:S(2)}, u32[]{:S(2)}) collective-permute-start(f32[128,1152]{1,0:T(8,128)} %get-tuple-element.69), channel_id=1, source_target_pairs={{0,6},{2,0},{4,2},{6,4},{1,7},{3,1},{5,3},{7,5},{8,14},{10,8},{12,... | collective-permute-start | bytes 1769480 | tf_op jit(solution)/shard_map/ppermute | solution.py:20
  12.4 15.6 %collective-permute-start.2 = (f32[128,1152]{1,0:T(8,128)}, f32[128,1152]{1,0:T(8,128)S(1)}, u32[]{:S(2)}, u32[]{:S(2)}) collective-permute-start(f32[128,1152]{1,0:T(8,128)} %get-tuple-element.69), channel_id=1, source_target_pairs={{0,2},{2,4},{4,6},{6,0},{1,3},{3,5},{5,7},{7,1},{8,10},{10,12},{12... | collective-permute-start | bytes 1769480 | tf_op jit(solution)/shard_map/ppermute | solution.py:20
  50.2 21.0 %collective-permute-start.13 = (f32[512,1152]{1,0:T(8,128)}, f32[512,1152]{1,0:T(8,128)}, u32[]{:S(2)}, u32[]{:S(2)}) collective-permute-start(f32[512,1152]{1,0:T(8,128)} %constant_dynamic-update-slice_fusion.1.refs_8_), channel_id=1, source_target_pairs={{0,1},{1,0},{2,3},{3,2},{4,5},{5,4},{6,7},{7,6},{8,9},{9,8},{10,11... | collective-permute-start | bytes 7077896 | tf_op jit(solution)/shard_map/ppermute | solution.py:20
  50.2 17.0 %collective-permute-start.10 = (f32[128,1152]{1,0:T(8,128)S(1)}, f32[128,1152]{1,0:T(8,128)S(1)}, u32[]{:S(2)}, u32[]{:S(2)}) collective-permute-start(f32[128,1152]{1,0:T(8,128)S(1)} %collective-permute-done.5), channel_id=1, source_target_pairs={{0,2},{2,4},{4,6},{6,0},{1,3},{3,5},{5,7},{7,1},{8,10},{10,12},{12... | collective-permute-start | bytes 1769480 | tf_op jit(solution)/shard_map/ppermute | solution.py:20
  50.2 17.0 %collective-permute-start.12 = (f32[128,1152]{1,0:T(8,128)S(1)}, f32[128,1152]{1,0:T(8,128)S(1)}, u32[]{:S(2)}, u32[]{:S(2)}) collective-permute-start(f32[128,1152]{1,0:T(8,128)S(1)} %collective-permute-done.4.refs_1_), channel_id=1, source_target_pairs={{0,16},{16,32},{32,48},{48,0},{1,17},{17,33},{33,49},{49,1},{2,18}... | collective-permute-start | bytes 1769480 | tf_op jit(solution)/shard_map/ppermute | solution.py:20
  50.3 16.9 %collective-permute-start.9 = (f32[128,1152]{1,0:T(8,128)S(1)}, f32[128,1152]{1,0:T(8,128)S(1)}, u32[]{:S(2)}, u32[]{:S(2)}) collective-permute-start(f32[128,1152]{1,0:T(8,128)S(1)} %collective-permute-done.5), channel_id=1, source_target_pairs={{0,6},{2,0},{4,2},{6,4},{1,7},{3,1},{5,3},{7,5},{8,14},{10,8},{12,... | collective-permute-start | bytes 1769480 | tf_op jit(solution)/shard_map/ppermute | solution.py:20
  53.5 16.0 %collective-permute-start.11 = (f32[128,1152]{1,0:T(8,128)}, f32[128,1152]{1,0:T(8,128)}, u32[]{:S(2)}, u32[]{:S(2)}) collective-permute-start(f32[128,1152]{1,0:T(8,128)} %collective-permute-done.8.refs_6_), channel_id=1, source_target_pairs={{0,48},{16,0},{32,16},{48,32},{1,49},{17,1},{33,17},{49,33},{2,50}... | collective-permute-start | bytes 1769480 | tf_op jit(solution)/shard_map/ppermute | solution.py:20
  69.4 36.5 %collective-permute-start.14 = (f32[128,1152]{1,0:T(8,128)S(1)}, f32[128,1152]{1,0:T(8,128)S(1)}, u32[]{:S(2)}, u32[]{:S(2)}) collective-permute-start(f32[128,1152]{1,0:T(8,128)S(1)} %collective-permute-done.9), channel_id=1, source_target_pairs={{0,6},{2,0},{4,2},{6,4},{1,7},{3,1},{5,3},{7,5},{8,14},{10,8},{12,... | collective-permute-start | bytes 1769480 | tf_op jit(solution)/shard_map/ppermute | solution.py:20
  106.2 41.9 %collective-permute-start.18 = (f32[512,1152]{1,0:T(8,128)}, f32[512,1152]{1,0:T(8,128)S(1)}, u32[]{:S(2)}, u32[]{:S(2)}) collective-permute-start(f32[512,1152]{1,0:T(8,128)} %get-tuple-element.106), channel_id=1, source_target_pairs={{0,1},{1,0},{2,3},{3,2},{4,5},{5,4},{6,7},{7,6},{8,9},{9,8},{10,11... | collective-permute-start | bytes 7077896 | tf_op jit(solution)/shard_map/ppermute | solution.py:20
  148.3 18.1 %collective-permute-start.16 = (f32[128,1152]{1,0:T(8,128)}, f32[128,1152]{1,0:T(8,128)S(1)}, u32[]{:S(2)}, u32[]{:S(2)}) collective-permute-start(f32[128,1152]{1,0:T(8,128)} %get-tuple-element.103), channel_id=1, source_target_pairs={{0,16},{16,32},{32,48},{48,0},{1,17},{17,33},{33,49},{49,1},{2,18}... | collective-permute-start | bytes 1769480 | tf_op jit(solution)/shard_map/ppermute | solution.py:20
  148.3 18.1 %collective-permute-start.17 = (f32[128,1152]{1,0:T(8,128)}, f32[128,1152]{1,0:T(8,128)S(1)}, u32[]{:S(2)}, u32[]{:S(2)}) collective-permute-start(f32[128,1152]{1,0:T(8,128)} %get-tuple-element.104), channel_id=1, source_target_pairs={{0,48},{16,0},{32,16},{48,32},{1,49},{17,1},{33,17},{49,33},{2,50}... | collective-permute-start | bytes 1769480 | tf_op jit(solution)/shard_map/ppermute | solution.py:20
  155.1 15.4 %collective-permute-start.21 = (f32[128,1152]{1,0:T(8,128)S(1)}, f32[128,1152]{1,0:T(8,128)S(1)}, u32[]{:S(2)}, u32[]{:S(2)}) collective-permute-start(f32[128,1152]{1,0:T(8,128)S(1)} %get-tuple-element.136), channel_id=1, source_target_pairs={{0,6},{2,0},{4,2},{6,4},{1,7},{3,1},{5,3},{7,5},{8,14},{10,8},{12,... | collective-permute-start | bytes 1769480 | tf_op jit(solution)/shard_map/ppermute | solution.py:20
  156.1 16.3 %collective-permute-start.20 = (f32[128,1152]{1,0:T(8,128)S(1)}, f32[128,1152]{1,0:T(8,128)S(1)}, u32[]{:S(2)}, u32[]{:S(2)}) collective-permute-start(f32[128,1152]{1,0:T(8,128)S(1)} %get-tuple-element.137), channel_id=1, source_target_pairs={{0,2},{2,4},{4,6},{6,0},{1,3},{3,5},{5,7},{7,1},{8,10},{10,12},{12... | collective-permute-start | bytes 1769480 | tf_op jit(solution)/shard_map/ppermute | solution.py:20
  157.2 21.5 %collective-permute-start.23 = (f32[128,1152]{1,0:T(8,128)S(1)}, f32[128,1152]{1,0:T(8,128)S(1)}, u32[]{:S(2)}, u32[]{:S(2)}) collective-permute-start(f32[128,1152]{1,0:T(8,128)S(1)} %copy-done.14), channel_id=1, source_target_pairs={{0,16},{16,32},{32,48},{48,0},{1,17},{17,33},{33,49},{49,1},{2,18}... | collective-permute-start | bytes 1769480 | tf_op jit(solution)/shard_map/ppermute | solution.py:20
  175.7 16.3 %collective-permute-start.26 = (f32[128,1152]{1,0:T(8,128)S(1)}, f32[128,1152]{1,0:T(8,128)S(1)}, u32[]{:S(2)}, u32[]{:S(2)}) collective-permute-start(f32[128,1152]{1,0:T(8,128)S(1)} %get-tuple-element.134), channel_id=1, source_target_pairs={{0,6},{2,0},{4,2},{6,4},{1,7},{3,1},{5,3},{7,5},{8,14},{10,8},{12,... | collective-permute-start | bytes 1769480 | tf_op jit(solution)/shard_map/ppermute | solution.py:20
  175.9 16.1 %collective-permute-start.25 = (f32[128,1152]{1,0:T(8,128)S(1)}, f32[128,1152]{1,0:T(8,128)S(1)}, u32[]{:S(2)}, u32[]{:S(2)}) collective-permute-start(f32[128,1152]{1,0:T(8,128)S(1)} %get-tuple-element.135), channel_id=1, source_target_pairs={{0,2},{2,4},{4,6},{6,0},{1,3},{3,5},{5,7},{7,1},{8,10},{10,12},{12... | collective-permute-start | bytes 1769480 | tf_op jit(solution)/shard_map/ppermute | solution.py:20
  177.8 17.9 %collective-permute-start.22 = (f32[128,1152]{1,0:T(8,128)S(1)}, f32[128,1152]{1,0:T(8,128)S(1)}, u32[]{:S(2)}, u32[]{:S(2)}) collective-permute-start(f32[128,1152]{1,0:T(8,128)S(1)} %add.411), channel_id=1, source_target_pairs={{0,16},{16,32},{32,48},{48,0},{1,17},{17,33},{33,49},{49,1},{2,18}... | collective-permute-start | bytes 1769480 | tf_op jit(solution)/shard_map/ppermute | solution.py:20
  178.7 23.8 %collective-permute-start.30 = (f32[128,1152]{1,0:T(8,128)}, f32[128,1152]{1,0:T(8,128)}, u32[]{:S(2)}, u32[]{:S(2)}) collective-permute-start(f32[128,1152]{1,0:T(8,128)} %slice.42), channel_id=1, source_target_pairs={{0,6},{2,0},{4,2},{6,4},{1,7},{3,1},{5,3},{7,5},{8,14},{10,8},{12,... | collective-permute-start | bytes 1769480 | tf_op jit(solution)/shard_map/ppermute | solution.py:20
  193.7 18.1 %collective-permute-start.31 = (f32[128,1152]{1,0:T(8,128)}, f32[128,1152]{1,0:T(8,128)}, u32[]{:S(2)}, u32[]{:S(2)}) collective-permute-start(f32[128,1152]{1,0:T(8,128)} %get-tuple-element.133), channel_id=1, source_target_pairs={{0,8},{8,0},{1,9},{9,1},{2,10},{10,2},{3,11},{11,3},{4,12},{12,4},... | collective-permute-start | bytes 1769480 | tf_op jit(solution)/shard_map/ppermute | solution.py:20
  195.3 22.2 %collective-permute-start.28 = (f32[128,1152]{1,0:T(8,128)}, f32[128,1152]{1,0:T(8,128)}, u32[]{:S(2)}, u32[]{:S(2)}) collective-permute-start(f32[128,1152]{1,0:T(8,128)} %add_add_fusion), channel_id=1, source_target_pairs={{0,64},{64,0},{1,65},{65,1},{2,66},{66,2},{3,67},{67,3},{4,68},{68... | collective-permute-start | bytes 1769480 | tf_op jit(solution)/shard_map/ppermute | solution.py:20
  196.5 20.9 %collective-permute-start.27 = (f32[128,1152]{1,0:T(8,128)}, f32[128,1152]{1,0:T(8,128)}, u32[]{:S(2)}, u32[]{:S(2)}) collective-permute-start(f32[128,1152]{1,0:T(8,128)} %get-tuple-element.117), channel_id=1, source_target_pairs={{0,48},{16,0},{32,16},{48,32},{1,49},{17,1},{33,17},{49,33},{2,50}... | collective-permute-start | bytes 1769480 | tf_op jit(solution)/shard_map/ppermute | solution.py:20
  (24 other events, 321.1 us)
